TPU v7x, 512 devices: a whole 4x8x8 slice. The times are simulated.
512 devices in a mesh: vox: 16 (over x, y_hi, core), vf: 32 (over y_lo, z).
Axes of the slice: x: 4, y: 8 (y_hi: 2, y_lo: 4; y = y_hi * 4 + y_lo), z: 8, core: 2. Of those that a mesh axis runs over, the one named last changes fastest.
Arguments:
- latents: bfloat16 [96, 1024, 1152], P('vf', 'vox'), may hold values from -6 to 6
- block_mask: int32 [96, 16, 32], P('vf', 'vox'), may hold values from 0 to 1, as said below
- occupancy: bfloat16 [32, 64, 512], P('vox'), may hold values from -6 to 6
- temporal_qkv: bfloat16 [1152, 1728], P('vox'), may hold values from -0.1875 to 0.1875
- temporal_out: bfloat16 [576, 1152], P('vox'), may hold values from -0.25 to 0.25
- cross_query: bfloat16 [1152, 576], P('vox'), may hold values from -0.1875 to 0.1875
- cross_keyval: bfloat16 [512, 1152], P('vox'), may hold values from -0.25 to 0.25
- cross_out: bfloat16 [576, 1152], P('vox'), may hold values from -0.25 to 0.25
Outputs:
- mixed_latents: bfloat16 [96, 1024, 1152], P('vf', 'vox')
Inputs may be any that keep to these rules, and one draw needn't show every extreme that they name: `block_mask`: every tile (r, b) attends between 1 and 8 voxel blocks, and some tile attends exactly 8.
All inputs are finite; a program needn't handle non-finite values.
Results may differ from a plain program's by a relative error of at most 0.0057.
Values may be sent and summed in bfloat16 or wider, within the bound.
No kernel may reach another device: no remote copies, remote signals or barrier semaphores. Data moves between devices by JAX's collectives and lax.ppermute only.
A program may use at most 128 MiB of HBM per device.

v0:
```python
import jax
import jax.numpy as jnp
from jax import lax
from jax.sharding import PartitionSpec as P

HEADS = 8
VIEWS = 6


epsilon = 1e-06


def rms_rows(values):
    return values * lax.rsqrt(jnp.mean(values * values, axis=-1, keepdims=True) + epsilon)


def head_normalize(values, head_count):
    shaped = values.reshape(values.shape[:-1] + (head_count, values.shape[-1] // head_count))
    return rms_rows(shaped).reshape(values.shape)


def slab_project(slab_rows, keyval_weight):
    block_count, block_width, channels = slab_rows.shape
    projected = jnp.dot(
        slab_rows.reshape(-1, channels), keyval_weight, preferred_element_type=jnp.float32
    )
    inner_width = keyval_weight.shape[1] // 2
    key_rows = head_normalize(projected[:, :inner_width], HEADS).astype(jnp.bfloat16)
    value_rows = projected[:, inner_width:].astype(jnp.bfloat16)
    return (
        key_rows.reshape(block_count, block_width, inner_width),
        value_rows.reshape(block_count, block_width, inner_width),
    )


def temporal_attend(query_rows, key_rows, value_rows, positions):
    inner_width = query_rows.shape[1]
    head_size = inner_width // HEADS

    def to_heads(tensor):
        return tensor.reshape(VIEWS, -1, positions, HEADS, head_size)

    scores = jnp.einsum(
        "vfphd,vgphd->vphfg",
        to_heads(query_rows),
        to_heads(key_rows),
        preferred_element_type=jnp.float32,
    ) * head_size ** (-0.5)
    exponent = jnp.exp(scores)
    probabilities = (exponent / jnp.sum(exponent, axis=-1, keepdims=True)).astype(jnp.bfloat16)
    mixed = jnp.einsum(
        "vphfg,vgphd->vfphd",
        probabilities,
        to_heads(value_rows),
        preferred_element_type=jnp.float32,
    )
    return mixed.astype(jnp.bfloat16).reshape(-1, inner_width)


def cross_attend(query_rows, tile_mask, slab_keys, slab_values):
    tile_count, positions, head_count, head_size = query_rows.shape
    blocks = slab_keys.shape[0]
    block_width = slab_keys.shape[1]
    most_blocks = blocks // 4
    ranking = tile_mask * blocks + (blocks - 1 - jnp.arange(blocks, dtype=jnp.int32))[None, :]
    chosen = lax.top_k(ranking, most_blocks)[1]
    live_blocks = jnp.take_along_axis(tile_mask, chosen, axis=1)
    picked_keys = slab_keys[chosen].reshape(
        tile_count, most_blocks * block_width, head_count, head_size
    )
    picked_values = slab_values[chosen].reshape(
        tile_count, most_blocks * block_width, head_count, head_size
    )
    key_live = jnp.repeat(live_blocks, block_width, axis=1).astype(jnp.float32)
    scores = jnp.einsum(
        "tphd,tkhd->thpk", query_rows, picked_keys, preferred_element_type=jnp.float32
    ) * head_size ** (-0.5)
    exponent = jnp.exp(scores) * key_live[:, None, None, :]
    probabilities = (exponent / jnp.sum(exponent, axis=-1, keepdims=True)).astype(jnp.bfloat16)
    mixed = jnp.einsum(
        "thpk,tkhd->tphd", probabilities, picked_values, preferred_element_type=jnp.float32
    )
    return mixed.astype(jnp.bfloat16).reshape(-1, head_count * head_size)


def shards(
    latents, block_mask, occupancy, temporal_qkv, temporal_out, cross_query, cross_keyval, cross_out
):
    tile_count, positions, model_width = latents.shape
    inner_width = cross_query.shape[1]
    head_size = inner_width // HEADS
    qkv_full, out_full, query_full, keyval_full, cross_full = (
        lax.all_gather(temporal_qkv, "vox", axis=0, tiled=True),
        lax.all_gather(temporal_out, "vox", axis=0, tiled=True),
        lax.all_gather(cross_query, "vox", axis=0, tiled=True),
        lax.all_gather(cross_keyval, "vox", axis=0, tiled=True),
        lax.all_gather(cross_out, "vox", axis=0, tiled=True),
    )
    time_rows = lax.all_to_all(latents, "vf", split_axis=1, concat_axis=0, tiled=True)
    local_positions = time_rows.shape[1]
    time_flat = time_rows.reshape(-1, model_width)
    normed = rms_rows(time_flat.astype(jnp.float32)).astype(jnp.bfloat16)
    projected = jnp.dot(normed, qkv_full, preferred_element_type=jnp.float32)
    query_rows = head_normalize(projected[:, :inner_width], HEADS).astype(jnp.bfloat16)
    key_rows = head_normalize(projected[:, inner_width : 2 * inner_width], HEADS).astype(
        jnp.bfloat16
    )
    value_rows = projected[:, 2 * inner_width :].astype(jnp.bfloat16)
    temporal_mixed = temporal_attend(query_rows, key_rows, value_rows, local_positions)
    hidden_time = (
        time_flat.astype(jnp.float32)
        + jnp.dot(temporal_mixed, out_full, preferred_element_type=jnp.float32)
    ).astype(jnp.bfloat16)
    hidden = lax.all_to_all(
        hidden_time.reshape(time_rows.shape), "vf", split_axis=0, concat_axis=1, tiled=True
    ).reshape(-1, model_width)
    own_keys, own_values = slab_project(occupancy, keyval_full)
    slab_keys, slab_values = (
        lax.all_gather(own_keys, "vox", axis=0, tiled=True),
        lax.all_gather(own_values, "vox", axis=0, tiled=True),
    )
    hidden_normed = rms_rows(hidden.astype(jnp.float32)).astype(jnp.bfloat16)
    cross_rows = jnp.dot(hidden_normed, query_full, preferred_element_type=jnp.float32)
    cross_rows = head_normalize(cross_rows, HEADS).astype(jnp.bfloat16)
    cross_rows = cross_rows.reshape(tile_count, positions, HEADS, head_size)
    crossed = cross_attend(cross_rows, block_mask[:, 0, :], slab_keys, slab_values)
    result = (
        hidden.astype(jnp.float32)
        + jnp.dot(crossed, cross_full, preferred_element_type=jnp.float32)
    ).astype(jnp.bfloat16)
    return result.reshape(tile_count, positions, model_width)


def solution(mesh):
    return jax.shard_map(
        shards,
        mesh=mesh,
        in_specs=(
            P("vf", "vox", None),
            P("vf", "vox", None),
            P("vox", None, None),
            P("vox", None),
            P("vox", None),
            P("vox", None),
            P("vox", None),
            P("vox", None),
        ),
        out_specs=P("vf", "vox", None),
        check_vma=False,
    )
```

profile of v0, /device:TPU:1, one launch (start us, length us, event | category | flops | bytes accessed | tf_op | source)
XLA Modules:
  0.0 526.9 jit_solution(14762366255644268102)
XLA Ops:
  10.0 66.9 %all-gather.12.cloned.1.call-done = bf16[512,1152]{1,0:T(8,128)(2,1)} async-done(((bf16[32,1152]{1,0:T(8,128)(2,1)}), bf16[512,1152]{1,0:T(8,128)(2,1)}) %all-gather.12.cloned.1.call-update) | async-done | bytes 1179664 | tf_op jit(solution)/shard_map/all_gather | solution.py:96
  80.9 9.1 %all-to-all-start = ((bf16[3,64,1152]{2,0,1:T(4,128)(2,1)}), bf16[3,64,1152]{2,0,1:T(4,128)(2,1)S(1)}, u32[]{:S(2)}, u32[]{:S(2)}) async-start(bf16[3,64,1152]{2,0,1:T(4,128)(2,1)} %copy.124), calls=%async_computation | async-start | bytes 1179648 | tf_op jit(solution)/shard_map/all_to_all | solution.py:99
  90.9 17.8 %all-to-all-done = bf16[3,64,1152]{2,0,1:T(4,128)(2,1)S(1)} async-done(((bf16[3,64,1152]{2,0,1:T(4,128)(2,1)}), bf16[3,64,1152]{2,0,1:T(4,128)(2,1)S(1)}, u32[]{:S(2)}, u32[]{:S(2)}) %all-to-all-start) | async-done | bytes 442400 | tf_op jit(solution)/shard_map/all_to_all | solution.py:99
  110.5 30.8 %all-gather.20.cloned.1.call-done = bf16[16,36,1152]{2,1,0:T(8,128)(2,1)} async-done(((bf16[1,36,1152]{2,1,0:T(8,128)(2,1)}), bf16[16,36,1152]{2,1,0:T(8,128)(2,1)}) %all-gather.20.cloned.1.call-update) | async-done | bytes 1327120 | tf_op jit(solution)/shard_map/all_gather | solution.py:94
  141.4 3.3 reshape.213
  144.6 79.6 %all-gather.10.cloned.1.call-done = bf16[1152,1728]{1,0:T(8,128)(2,1)} async-done(((bf16[72,1728]{1,0:T(8,128)(2,1)}), bf16[1152,1728]{1,0:T(8,128)(2,1)}) %all-gather.10.cloned.1.call-update) | async-done | bytes 3981328 | tf_op jit(solution)/shard_map/all_gather | solution.py:93
  224.2 3.3 fusion.18
  232.3 1.9 multiply_convert_fusion.4
  240.8 8.0 %all-to-all-start.1 = ((bf16[96,2,1152]{2,1,0:T(2,128)(2,1)}), bf16[96,2,1152]{2,1,0:T(2,128)(2,1)}, u32[]{:S(2)}, u32[]{:S(2)}) async-start(bf16[96,2,1152]{2,1,0:T(2,128)(2,1)} %reshape.161), calls=%async_computation.1 | async-start | bytes 884736 | tf_op jit(solution)/shard_map/all_to_all | solution.py:114
  251.3 34.4 %all-gather.16.cloned.1.call-done = bf16[1152,576]{1,0:T(8,128)(2,1)} async-done(((bf16[72,576]{1,0:T(8,128)(2,1)}), bf16[1152,576]{1,0:T(8,128)(2,1)}) %all-gather.16.cloned.1.call-update) | async-done | bytes 1327120 | tf_op jit(solution)/shard_map/all_gather | solution.py:95
  285.7 2.6 copy.140
  288.3 60.3 %all-gather.22.cloned.1.call-done = bf16[16,36,1152]{2,1,0:T(8,128)(2,1)} async-done(((bf16[1,36,1152]{2,1,0:T(8,128)(2,1)}), bf16[16,36,1152]{2,1,0:T(8,128)(2,1)}) %all-gather.22.cloned.1.call-update) | async-done | bytes 1327120 | tf_op jit(solution)/shard_map/all_gather | solution.py:97
  348.6 3.2 reshape.215
  351.9 67.7 %all-gather.18.cloned.1.call-done = bf16[32,64,576]{2,1,0:T(8,128)(2,1)} async-done(((bf16[2,64,576]{2,1,0:T(8,128)(2,1)}), bf16[32,64,576]{2,1,0:T(8,128)(2,1)}) %all-gather.18.cloned.1.call-update) | async-done | bytes 2359312 | tf_op jit(solution)/shard_map/all_gather | solution.py:119
  419.6 3.9 gather_fusion.1
  423.5 5.0 reshape.166
  428.6 62.0 %all-gather.14.cloned.1.call-done = bf16[32,64,576]{2,1,0:T(8,128)(2,1)} async-done(((bf16[2,64,576]{2,1,0:T(8,128)(2,1)}), bf16[32,64,576]{2,1,0:T(8,128)(2,1)}) %all-gather.14.cloned.1.call-update) | async-done | bytes 2359312 | tf_op jit(solution)/shard_map/all_gather | solution.py:120
  490.6 4.0 gather_fusion
  494.6 6.3 %reshape.164 = bf16[3,512,8,72]{3,2,1,0:T(8,128)(2,1)} reshape(bf16[24,64,576]{2,1,0:T(8,128)(2,1)} %gather_fusion) | data formatting | bytes 3538944 | tf_op jit(solution)/shard_map/reshape | solution.py:71
  502.5 2.2 copy_bitcast_fusion
  504.7 2.2 multiply_convert_fusion
  506.9 1.9 reshape.216
  508.9 2.0 multiply_reduce_fusion.2
  513.6 2.6 fusion.4
  (99 shorter events, 31.7 us)
Async XLA Ops:
  6.5 70.4 %copy-start = (bf16[2,64,512]{2,1,0:T(8,128)(2,1)S(1)}, bf16[2,64,512]{2,1,0:T(8,128)(2,1)}, u32[]{:S(2)}) copy-start(bf16[2,64,512]{2,1,0:T(8,128)(2,1)} %param.10) | copy-start | bytes 393220
  6.5 70.4 %all-gather.12.cloned.1.call-start = ((), (), s32[]{:S(2)}) async-start(), calls=%async_computation.3 | async-start | bytes 1253376 | tf_op jit(solution)/shard_map/all_gather | solution.py:96
  7.3 134.1 %all-gather.20.cloned.1.call-start = ((), (), s32[]{:S(2)}) async-start(), calls=%async_computation.7 | async-start | bytes 1566720 | tf_op jit(solution)/shard_map/all_gather | solution.py:94
  8.0 216.2 %all-gather.10.cloned.1.call-start = ((), (), s32[]{:S(2)}) async-start(), calls=%async_computation.2 | async-start | bytes 4386816 | tf_op jit(solution)/shard_map/all_gather | solution.py:93
  8.7 277.0 %all-gather.16.cloned.1.call-start = ((), (), s32[]{:S(2)}) async-start(), calls=%async_computation.5 | async-start | bytes 1566720 | tf_op jit(solution)/shard_map/all_gather | solution.py:95
  9.3 339.3 %all-gather.22.cloned.1.call-start = ((), (), s32[]{:S(2)}) async-start(), calls=%async_computation.8 | async-start | bytes 1566720 | tf_op jit(solution)/shard_map/all_gather | solution.py:97
  9.9 409.7 %all-gather.18.cloned.1.call-start = ((), (), s32[]{:S(2)}) async-start(), calls=%async_computation.6 | async-start | bytes 2785280 | tf_op jit(solution)/shard_map/all_gather | solution.py:119
  78.5 1.1 copy-start.6
  80.9 27.7 %all-to-all-start = ((bf16[3,64,1152]{2,0,1:T(4,128)(2,1)}), bf16[3,64,1152]{2,0,1:T(4,128)(2,1)S(1)}, u32[]{:S(2)}, u32[]{:S(2)}) async-start(bf16[3,64,1152]{2,0,1:T(4,128)(2,1)} %copy.124), calls=%async_computation | async-start | bytes 1179648 | tf_op jit(solution)/shard_map/all_to_all | solution.py:99
  90.0 400.6 %all-gather.14.cloned.1.call-start = ((), (), s32[]{:S(2)}) async-start(), calls=%async_computation.4 | async-start | bytes 2785280 | tf_op jit(solution)/shard_map/all_gather | solution.py:120
  232.3 3.7 copy-start.5
  236.7 2.5 copy-start.2
  239.3 9.5 %copy-start.7 = (s32[3,1,32]{2,1,0:T(1,128)S(1)}, s32[3,1,32]{2,1,0:T(1,128)}, u32[]{:S(2)}) copy-start(s32[3,1,32]{2,1,0:T(1,128)} %param.9) | copy-start | bytes 1156
  240.8 260.1 %all-to-all-start.1 = ((bf16[96,2,1152]{2,1,0:T(2,128)(2,1)}), bf16[96,2,1152]{2,1,0:T(2,128)(2,1)}, u32[]{:S(2)}, u32[]{:S(2)}) async-start(bf16[96,2,1152]{2,1,0:T(2,128)(2,1)} %reshape.161), calls=%async_computation.1 | async-start | bytes 884736 | tf_op jit(solution)/shard_map/all_to_all | solution.py:114
  513.6 2.6 copy-start.4
  516.2 1.8 copy-start.3
  517.4 1.3 copy-start.1
Sparse Core Ops, SparseCore 0:
  10.6 66.2 all-gather.11
  80.3 61.0 all-gather.19
  144.6 79.5 all-gather.9
  227.5 58.1 all-gather.15
  288.9 59.6 all-gather.21
  351.8 67.8 all-gather.17
  422.9 67.6 all-gather.13
where the time goes:
time: 528 us; the launch traced here: 527 us
  waiting for transfers between devices  423 us (80%)
  local copies, waits for them, and re-layouts  47.7 us (9%)
  starting transfers between devices  17.3 us (3%)
  matrix products  14.1 us (3%)
  between operations  13.9 us (3%)
  other arithmetic  11.1 us (2%)
    all_gather x1, waiting for transfers between devices, shards(): lax.all_gather(temporal_qkv, 'vox', axis=0, tiled=True)  79.6 us
    all_gather x1, waiting for transfers between devices, shards(): lax.all_gather(own_keys, 'vox', axis=0, tiled=True)  67.7 us
    all_gather x1, waiting for transfers between devices, shards(): lax.all_gather(cross_keyval, 'vox', axis=0, tiled=True)  66.9 us
    all_gather x1, waiting for transfers between devices, shards(): lax.all_gather(own_values, 'vox', axis=0, tiled=True)  62 us
    all_gather x1, waiting for transfers between devices, shards(): lax.all_gather(cross_out, 'vox', axis=0, tiled=True)  60.3 us
    all_gather x1, waiting for transfers between devices, shards(): lax.all_gather(cross_query, 'vox', axis=0, tiled=True)  34.4 us
    all_gather x1, waiting for transfers between devices, shards(): lax.all_gather(temporal_out, 'vox', axis=0, tiled=True)  30.8 us
    all_to_all x1, waiting for transfers between devices, shards(): lax.all_to_all(latents, 'vf', split_axis=1, concat_axis=0, tiled=True)  17.8 us
  transfers between devices with their start and end apart: 9, of which 8 were waited for; matrix products, arithmetic and copies ran while one was open for 10% of the time, Pallas kernels for 0%

commit v1 on v0

v1 whole, which is shorter than its diff:
```python
import functools

import jax
import jax.numpy as jnp
from jax import lax
from jax.experimental import pallas as pl
from jax.experimental.pallas import tpu as pltpu
from jax.sharding import Mesh
from jax.sharding import PartitionSpec as P

HEADS = 8
HEAD = 72
INNER = 576
WIDTH = 1152
CHANNELS = 512
EPS = 1e-06
SCALE = HEAD ** (-0.5)
BF = jnp.bfloat16
F32 = jnp.float32

OUT_AT, CO_AT, KV_AT, PACK = 128, 176, 224, 256
CQ_LANE = 512
VMEM = 60 * 1024 * 1024


def mm(a, b):
    return lax.dot_general(a, b, (((1,), (0,)), ((), ())), preferred_element_type=F32)


def mm_nt(a, b):
    return lax.dot_general(a, b, (((1,), (1,)), ((), ())), preferred_element_type=F32)


def iota(shape, dim):
    return lax.broadcasted_iota(jnp.int32, shape, dim)


def onehot(hit):
    return jnp.where(hit, 1.0, 0.0).astype(BF)


def split_mm(a, b):
    high = a.astype(BF)
    low = (a - high.astype(F32)).astype(BF)
    return mm(high, b) + mm(low, b)


def head_normalize(values):
    width = values.shape[1]
    gather = onehot(iota((width, 128), 0) // HEAD == iota((width, 128), 1))
    spread = onehot(iota((128, width), 1) // HEAD == iota((128, width), 0))
    mean = split_mm(values * values, gather) * (1.0 / HEAD)
    return values * split_mm(lax.rsqrt(mean + EPS), spread)


def rms_rows(values):
    return values * lax.rsqrt(jnp.mean(values * values, axis=-1, keepdims=True) + EPS)


def head_masked(rows):
    head = iota(rows.shape, 1) // HEAD
    return jnp.concatenate([jnp.where(head == h, rows, 0.0).astype(BF) for h in range(HEADS)], axis=0)


def head_merged(rows, count):
    head = iota((count, INNER), 1) // HEAD
    total = jnp.where(head == 0, rows[:count], 0.0)
    for h in range(1, HEADS):
        total = jnp.where(head == h, rows[h * count:(h + 1) * count], total)
    return total


def pack_kernel(occ_ref, cq_ref, out_ref, co_ref, kv_ref, packed_ref):
    packed_ref[...] = jnp.zeros(packed_ref.shape, BF)
    to = iota((CHANNELS, CHANNELS), 1)
    yh, x, c, r = to // 256, (to // 64) % 4, (to // 32) % 2, to % 32
    spread = onehot(iota((CHANNELS, CHANNELS), 0) == (x * 4 + yh * 2 + c) * 32 + r)
    packed_ref[0:128, 0:CHANNELS] = mm(occ_ref[...], spread).astype(BF)
    packed_ref[0:72, CQ_LANE:CQ_LANE + INNER] = cq_ref[...]
    packed_ref[OUT_AT:OUT_AT + 36, :] = out_ref[...]
    packed_ref[CO_AT:CO_AT + 36, :] = co_ref[...]
    packed_ref[KV_AT:KV_AT + 32, :] = kv_ref[...]


def send_kernel(lat_ref, sent_ref):
    to, src = iota((256, 192), 0), iota((256, 192), 1)
    j, i, p = to // 16, (to // 4) % 4, to % 4
    pick = onehot((src == i * 64 + j * 4 + p) & (i < 3))
    sent_ref[...] = mm(pick, lat_ref[...]).astype(BF)


def prep_kernel(rows_ref, index_ref, normed_ref):
    to, src = iota((192, 256), 0), iota((192, 256), 1)
    pick = onehot(src == (to // 12) * 16 + to % 12)
    rows = mm(pick, rows_ref[...])
    normed = rms_rows(rows).astype(BF)
    for k in range(4):
        spread = onehot(iota((WIDTH, 384), 0) == index_ref[:, k * 384:(k + 1) * 384])
        normed_ref[:, k * 384:(k + 1) * 384] = mm(normed, spread).astype(BF)


def temporal_kernel(normed_ref, a4_ref, a8_ref, b4_ref, b8_ref, mixed_ref):
    projected = None
    for k, w_ref in enumerate((a4_ref, a8_ref, b4_ref, b8_ref)):
        term = mm(normed_ref[:, k * 384:k * 384 + 288], w_ref[...])
        projected = term if projected is None else projected + term
    both = head_normalize(projected[:, :2 * INNER])
    query = both[:, :INNER]
    key = both[:, INNER:].astype(BF)
    value = projected[:, 2 * INNER:].astype(BF)
    live = iota((HEADS * 64, 64), 0) % 4 == iota((HEADS * 64, 64), 1) % 4
    mixed = []
    for view in range(3):
        rows = slice(view * 64, view * 64 + 64)
        scores = mm_nt(head_masked(query[rows]), key[rows]) * SCALE
        exponent = jnp.where(live, jnp.exp(scores), 0.0)
        weights = (exponent / jnp.sum(exponent, axis=-1, keepdims=True)).astype(BF)
        mixed.append(head_merged(mm(weights, value[rows]), 64).astype(BF))
    to, src = iota((256, 192), 0), iota((256, 192), 1)
    pick = onehot((src == (to // 16) * 12 + to % 16) & (to % 16 < 12))
    mixed_ref[...] = mm(pick, jnp.concatenate(mixed, axis=0)).astype(BF)


def slab_kernel(yh_ref, a_ref, b_ref, key_ref, value_ref):
    wa = a_ref[:, KV_AT:KV_AT + 32, :].reshape(256, WIDTH)
    wb = b_ref[:, KV_AT:KV_AT + 32, :].reshape(256, WIDTH)
    first = yh_ref[0] == 0
    w0 = jnp.where(first, wa, wb)
    w1 = jnp.where(first, wb, wa)
    for side, ref in enumerate((a_ref, b_ref)):
        for part in range(4):
            occ = ref[2 * part:2 * part + 2, 0:128, 0:CHANNELS].reshape(256, CHANNELS)
            projected = mm(occ[:, :256], w0) + mm(occ[:, 256:], w1)
            rows = slice(side * 1024 + part * 256, side * 1024 + part * 256 + 256)
            key_ref[rows, :] = head_normalize(projected[:, :INNER]).astype(BF)
            value_ref[rows, :] = projected[:, INNER:].astype(BF)


def cross_kernel(ids_ref, lat_ref, mixed_ref, live_ref, cols36_ref, cols72_ref, a_ref, b_ref,
                 key_ref, value_ref, result_ref):
    to, src = iota((192, 256), 0), iota((192, 256), 1)
    i, j, p = to // 64, (to % 64) // 4, to % 4
    pick = onehot(src == j * 16 + i * 4 + p)
    mixed = mm(pick, mixed_ref[...]).astype(BF)
    spread36 = onehot(iota((INNER, 768), 0) == cols36_ref[...])

    def out_project(rows, at):
        spread = mm(rows, spread36).astype(BF)
        return mm(spread[:, :384], a_ref[:, at:at + 48, :].reshape(384, WIDTH)) + mm(
            spread[:, 384:], b_ref[:, at:at + 48, :].reshape(384, WIDTH)
        )

    hidden = (lat_ref[...].astype(F32) + out_project(mixed, OUT_AT)).astype(BF)
    normed = rms_rows(hidden.astype(F32)).astype(BF)
    query = None
    for side, ref in enumerate((a_ref, b_ref)):
        spread72 = onehot(iota((WIDTH, 640), 0) == cols72_ref[:, side * 640:side * 640 + 640])
        columns = mm(normed, spread72).astype(BF)
        term = mm(columns, ref[:, 0:80, CQ_LANE:CQ_LANE + INNER].reshape(640, INNER))
        query = term if query is None else query + term
    query = head_normalize(query)
    crossed = []
    for tile in range(3):
        rows = slice(tile * 64, tile * 64 + 64)
        picked = [pl.ds(pl.multiple_of(ids_ref[tile, s] * 64, 64), 64) for s in range(8)]
        keys = jnp.concatenate([key_ref[at, :] for at in picked], axis=0)
        values = jnp.concatenate([value_ref[at, :] for at in picked], axis=0)
        scores = mm_nt(head_masked(query[rows]), keys) * SCALE
        exponent = jnp.exp(scores) * live_ref[tile:tile + 1, :]
        weights = (exponent / jnp.sum(exponent, axis=-1, keepdims=True)).astype(BF)
        crossed.append(head_merged(mm(weights, values), 64).astype(BF))
    crossed = jnp.concatenate(crossed, axis=0)
    result_ref[...] = (hidden.astype(F32) + out_project(crossed, CO_AT)).astype(BF)


def call(kernel, shapes, count, scalars=(), flops=0, size=0):
    memory = [pltpu.SMEM if n in scalars else pltpu.VMEM for n in range(count)]
    return pl.pallas_call(
        kernel,
        out_shape=shapes,
        in_specs=[pl.BlockSpec(memory_space=m) for m in memory],
        out_specs=jax.tree.map(lambda _: pl.BlockSpec(memory_space=pltpu.VMEM), shapes),
        compiler_params=pltpu.CompilerParams(vmem_limit_bytes=VMEM),
        cost_estimate=pl.CostEstimate(flops=flops, bytes_accessed=size, transcendentals=0),
    )


def after(value, *others):
    return lax.optimization_barrier((value,) + others)[0]


SWAP = [(0, 1), (1, 0)]
STEPS = (0, 1, 3, 2)


def shift(block, step):
    return lax.ppermute(block, "x", [(i, (i + step) % 4) for i in range(4)])


def columns_of(slots, order, rows, size, pad):
    place = jnp.arange(pad, dtype=jnp.int32)
    parts = []
    for x, yh, c in order:
        start = ((x * 2 + yh) * 2 + c) * rows
        parts.append(jnp.where(place < rows, start + place, -1))
    flat = jnp.concatenate(parts)
    return flat.reshape(1, -1) if size is None else flat


def shards(latents, block_mask, occupancy, temporal_qkv, temporal_out, cross_query, cross_keyval, cross_out):
    x, yh, c = lax.axis_index("x"), lax.axis_index("yh"), lax.axis_index("c")
    shape = jax.ShapeDtypeStruct
    lat = latents.reshape(192, WIDTH)

    qkv_b = lax.ppermute(temporal_qkv, "yh", SWAP)
    qkv_a4 = jnp.stack([temporal_qkv] + [shift(temporal_qkv, s) for s in STEPS[1:]])
    sent = call(send_kernel, shape((256, WIDTH), BF), 1)(lat)
    time_rows = lax.all_to_all(
        sent.reshape(16, 16, WIDTH), ("l", "z"), split_axis=0, concat_axis=0, tiled=True
    ).reshape(256, WIDTH)
    qkv_b4 = jnp.stack([qkv_b] + [shift(qkv_b, s) for s in STEPS[1:]])
    qkv_a8 = lax.ppermute(qkv_a4, "c", SWAP)
    qkv_b8 = lax.ppermute(qkv_b4, "c", SWAP)

    packed = call(pack_kernel, shape((PACK, WIDTH), BF), 5)(
        occupancy.reshape(128, CHANNELS), cross_query, temporal_out, cross_out, cross_keyval
    )
    packed_b = lax.ppermute(after(packed, qkv_b, qkv_a4), "yh", SWAP)
    rest_a = lax.all_gather(packed, ("x", "c"), axis=0, tiled=False)
    rest_b = lax.all_gather(packed_b, ("x", "c"), axis=0, tiled=False)

    place = jnp.arange(384, dtype=jnp.int32)
    steps = jnp.array(STEPS, jnp.int32)
    source_x = (x - steps[jnp.minimum(place // 72, 3)] + 4) % 4
    index = []
    for dy, dc in ((0, 0), (0, 1), (1, 0), (1, 1)):
        start = ((source_x * 2 + (yh ^ dy)) * 2 + (c ^ dc)) * 72
        index.append(jnp.where(place < 288, start + place % 72, -1))
    index = jnp.concatenate(index).reshape(1, 1536)
    normed = call(prep_kernel, shape((192, 1536), BF), 2)(time_rows, index)
    mixed = call(temporal_kernel, shape((256, INNER), BF), 5)(
        normed, *[w.reshape(288, 1728) for w in (qkv_a4, qkv_a8, qkv_b4, qkv_b8)]
    )
    mixed_home = lax.all_to_all(
        mixed.reshape(16, 16, INNER), ("l", "z"), split_axis=0, concat_axis=0, tiled=True
    ).reshape(256, INNER)

    def columns(rows, pad):
        place = jnp.arange(16 * pad, dtype=jnp.int32)
        slot, row = place // pad, place % pad
        side, sx, sc = slot // 8, (slot // 2) % 4, slot % 2
        start = ((sx * 2 + (yh ^ side)) * 2 + sc) * rows
        return jnp.where(row < rows, start + row, -1).reshape(1, 16 * pad)

    mask = block_mask[:, 0, :]
    rank = jnp.cumsum(mask, axis=1) - 1
    block = jnp.arange(32, dtype=jnp.int32)
    vox, half = block // 2, block % 2
    stored = ((((vox // 2) % 2) ^ yh) * 8 + (vox // 4) * 2 + vox % 2) * 2 + half
    chosen = (rank[:, :, None] == jnp.arange(8, dtype=jnp.int32)) & (mask[:, :, None] > 0)
    ids = jnp.sum(jnp.where(chosen, stored[None, :, None], 0), axis=1).astype(jnp.int32)
    live = jnp.repeat(jnp.any(chosen, axis=1), 64, axis=1).astype(F32)

    keys, values = call(slab_kernel, (shape((2048, INNER), BF),) * 2, 3, scalars=(0,))(
        yh.reshape(1).astype(jnp.int32), rest_a, rest_b
    )
    result = call(cross_kernel, shape((192, WIDTH), BF), 10, scalars=(0,))(
        ids, lat, mixed_home, live, columns(36, 48), columns(72, 80), rest_a, rest_b, keys, values
    )
    return result.reshape(latents.shape)


def solution(mesh):
    split = Mesh(mesh.devices.reshape(4, 2, 2, 2, 2, 8), ("x", "yh", "c", "g", "l", "z"))
    vox, vf = ("x", "yh", "c"), ("g", "l", "z")
    return jax.shard_map(
        shards,
        mesh=split,
        in_specs=(
            P(vf, vox, None),
            P(vf, vox, None),
            P(vox, None, None),
            P(vox, None),
            P(vox, None),
            P(vox, None),
            P(vox, None),
            P(vox, None),
        ),
        out_specs=P(vf, vox, None),
        check_vma=False,
    )
```

time: 528 us -> 164 us (0.31)
  the two profiles are of different devices: /device:TPU:1 before, /device:TPU:62 now
where the time goes in v1:
time: 164 us; the launch traced here: 163 us
  starting transfers between devices  51.8 us (32%)
  waiting for transfers between devices  46.6 us (28%)
  Pallas kernels  41.9 us (26%)
  between operations  13.6 us (8%)
  other arithmetic  4.71 us (3%)
  local copies, waits for them, and re-layouts  4.44 us (3%)
    ppermute x1, waiting for transfers between devices, shards(): packed_b = lax.ppermute(after(packed, qkv_b, qkv_a4), 'yh', SWAP)  25.6 us
    ppermute x6, starting transfers between devices, shift(): return lax.ppermute(block, 'x', [(i, (i + step) % 4) for i in range(4)])  21.2 us
    pallas_call x1, Pallas kernels, shards(): call(cross_kernel, shape((192, WIDTH), BF), 10, scalars=(0,))  14 us
    pallas_call x1, Pallas kernels, shards(): call(slab_kernel, (shape((2048, INNER), BF),) * 2, 3, scalars=(0,))  12.5 us
    all_to_all x1, starting transfers between devices, shards(): lax.all_to_all(sent.reshape(16, 16, WIDTH), ('l', 'z'), split_axis=0, con...  12 us
    ppermute x1, waiting for transfers between devices, shards(): qkv_b = lax.ppermute(temporal_qkv, 'yh', SWAP)  8.74 us
    all_to_all x1, waiting for transfers between devices, shards(): lax.all_to_all(sent.reshape(16, 16, WIDTH), ('l', 'z'), split_axis=0, con...  7.97 us
    pallas_call x1, Pallas kernels, shards(): call(temporal_kernel, shape((256, INNER), BF), 5)  7.65 us
  transfers between devices with their start and end apart: 14, of which 4 were waited for; matrix products, arithmetic and copies ran while one was open for 4% of the time, Pallas kernels for 16%

profile of v1, /device:TPU:62, one launch (start us, length us, event | category | flops | bytes accessed | tf_op | source)
XLA Modules:
  0.0 163.1 jit_solution(1512777332022126280)
XLA Ops:
  6.5 2.2 %shard_map.94 = bf16[256,1152]{1,0:T(8,128)(2,1)} custom-call(bf16[128,512]{1,0:T(8,128)(2,1)} %bitcast.47, bf16[72,576]{1,0:T(8,128)(2,1)} %cq_ref.1, bf16[36,1152]{1,0:T(8,128)(2,1)} %out_ref.1, bf16[36,1152]{1,0:T(8,128)(2,1)} %co_ref.1, bf16[32,1152]{1,0:T(8,128)(2,1)} %kv_ref.1), custom_call_target="tpu_custom_call" | custom-call | tf_op jit(solution)/shard_map/pallas_call | solution.py:225
  8.8 2.7 %collective-permute-start.1 = (bf16[72,1728]{1,0:T(8,128)(2,1)}, bf16[72,1728]{1,0:T(8,128)(2,1)S(1)}, u32[]{:S(2)}, u32[]{:S(2)}) collective-permute-start(bf16[72,1728]{1,0:T(8,128)(2,1)} %param.12), channel_id=1, source_target_pairs={{0,384},{128,0},{256,128},{384,256},{1,385},{129,1},{257,129},{385... | collective-permute-start | bytes 746504 | tf_op jit(solution)/shard_map/ppermute | solution.py:197
  11.5 4.3 %collective-permute-start = (bf16[72,1728]{1,0:T(8,128)(2,1)}, bf16[72,1728]{1,0:T(8,128)(2,1)S(1)}, u32[]{:S(2)}, u32[]{:S(2)}) collective-permute-start(bf16[72,1728]{1,0:T(8,128)(2,1)} %param.12), channel_id=1, source_target_pairs={{0,128},{128,256},{256,384},{384,0},{1,129},{129,257},{257,385},{3... | collective-permute-start | bytes 746504 | tf_op jit(solution)/shard_map/ppermute | solution.py:197
  15.9 2.1 %collective-permute-start.2 = (bf16[72,1728]{1,0:T(8,128)(2,1)}, bf16[72,1728]{1,0:T(8,128)(2,1)S(1)}, u32[]{:S(2)}, u32[]{:S(2)}) collective-permute-start(bf16[72,1728]{1,0:T(8,128)(2,1)} %param.12), channel_id=1, source_target_pairs={{0,256},{128,384},{256,0},{384,128},{1,257},{129,385},{257,1},{385... | collective-permute-start | bytes 746504 | tf_op jit(solution)/shard_map/ppermute | solution.py:197
  18.0 4.7 %collective-permute-start.4 = (bf16[72,1728]{1,0:T(8,128)(2,1)}, bf16[72,1728]{1,0:T(8,128)(2,1)S(1)}, u32[]{:S(2)}, u32[]{:S(2)}) collective-permute-start(bf16[72,1728]{1,0:T(8,128)(2,1)} %param.12), channel_id=1, source_target_pairs={{0,64},{64,0},{1,65},{65,1},{2,66},{66,2},{3,67},{67,3},{4,68},{68... | collective-permute-start | bytes 746504 | tf_op jit(solution)/shard_map/ppermute | solution.py:215
  22.7 4.2 %collective-permute-done = bf16[72,1728]{1,0:T(8,128)(2,1)S(1)} collective-permute-done((bf16[72,1728]{1,0:T(8,128)(2,1)}, bf16[72,1728]{1,0:T(8,128)(2,1)S(1)}, u32[]{:S(2)}, u32[]{:S(2)}) %collective-permute-start) | collective-permute-done | bytes 248864 | tf_op jit(solution)/shard_map/ppermute | solution.py:197
  26.9 1.1 pad_maximum_fusion
  28.0 8.7 %collective-permute-done.4 = bf16[72,1728]{1,0:T(8,128)(2,1)S(1)} collective-permute-done((bf16[72,1728]{1,0:T(8,128)(2,1)}, bf16[72,1728]{1,0:T(8,128)(2,1)S(1)}, u32[]{:S(2)}, u32[]{:S(2)}) %collective-permute-start.4) | collective-permute-done | bytes 248864 | tf_op jit(solution)/shard_map/ppermute | solution.py:215
  36.8 4.0 %collective-permute-start.9 = (bf16[256,1152]{1,0:T(8,128)(2,1)}, bf16[256,1152]{1,0:T(8,128)(2,1)S(1)}, u32[]{:S(2)}, u32[]{:S(2)}) collective-permute-start(bf16[256,1152]{1,0:T(8,128)(2,1)} %shard_map.94), channel_id=1, source_target_pairs={{0,64},{64,0},{1,65},{65,1},{2,66},{66,2},{3,67},{67,3},{4,68},{68... | collective-permute-start | bytes 1769480 | tf_op jit(solution)/shard_map/ppermute | solution.py:228
  40.8 25.6 %collective-permute-done.9 = bf16[256,1152]{1,0:T(8,128)(2,1)S(1)} collective-permute-done((bf16[256,1152]{1,0:T(8,128)(2,1)}, bf16[256,1152]{1,0:T(8,128)(2,1)S(1)}, u32[]{:S(2)}, u32[]{:S(2)}) %collective-permute-start.9) | collective-permute-done | bytes 589856 | tf_op jit(solution)/shard_map/ppermute | solution.py:228
  67.3 5.0 %collective-permute-start.7 = (bf16[72,1728]{1,0:T(8,128)(2,1)S(1)}, bf16[72,1728]{1,0:T(8,128)(2,1)S(1)}, u32[]{:S(2)}, u32[]{:S(2)}) collective-permute-start(bf16[72,1728]{1,0:T(8,128)(2,1)S(1)} %collective-permute-done.4), channel_id=1, source_target_pairs={{0,256},{128,384},{256,0},{384,128},{1,257},{129,385},{257,1},{385... | collective-permute-start | bytes 746504 | tf_op jit(solution)/shard_map/ppermute | solution.py:197
  72.3 1.9 %collective-permute-start.6 = (bf16[72,1728]{1,0:T(8,128)(2,1)S(1)}, bf16[72,1728]{1,0:T(8,128)(2,1)S(1)}, u32[]{:S(2)}, u32[]{:S(2)}) collective-permute-start(bf16[72,1728]{1,0:T(8,128)(2,1)S(1)} %collective-permute-done.4), channel_id=1, source_target_pairs={{0,384},{128,0},{256,128},{384,256},{1,385},{129,1},{257,129},{385... | collective-permute-start | bytes 746504 | tf_op jit(solution)/shard_map/ppermute | solution.py:197
  74.2 5.1 %collective-permute-start.5 = (bf16[72,1728]{1,0:T(8,128)(2,1)S(1)}, bf16[72,1728]{1,0:T(8,128)(2,1)S(1)}, u32[]{:S(2)}, u32[]{:S(2)}) collective-permute-start(bf16[72,1728]{1,0:T(8,128)(2,1)S(1)} %collective-permute-done.4), channel_id=1, source_target_pairs={{0,128},{128,256},{256,384},{384,0},{1,129},{129,257},{257,385},{3... | collective-permute-start | bytes 746504 | tf_op jit(solution)/shard_map/ppermute | solution.py:197
  79.4 2.2 %shard_map.91 = bf16[256,1152]{1,0:T(8,128)(2,1)} custom-call(bf16[192,1152]{1,0:T(8,128)(2,1)} %bitcast.35), custom_call_target="tpu_custom_call" | custom-call | tf_op jit(solution)/shard_map/pallas_call | solution.py:217
  81.5 12.0 %all-to-all-start = ((bf16[16,16,1152]{2,1,0:T(8,128)(2,1)}), bf16[16,16,1152]{2,1,0:T(8,128)(2,1)S(1)}, u32[]{:S(2)}, u32[]{:S(2)}) async-start(bf16[16,16,1152]{2,1,0:T(8,128)(2,1)} %bitcast.34), calls=%async_computation | async-start | bytes 1179648 | tf_op jit(solution)/shard_map/all_to_all | solution.py:218
  93.5 1.9 %collective-permute-start.3 = (bf16[4,72,1728]{2,1,0:T(8,128)(2,1)S(1)}, bf16[4,72,1728]{2,1,0:T(8,128)(2,1)}, u32[]{:S(2)}, u32[]{:S(2)}) collective-permute-start(bf16[4,72,1728]{2,1,0:T(8,128)(2,1)S(1)} %pad_maximum_fusion), channel_id=1, source_target_pairs={{0,32},{32,0},{1,33},{33,1},{2,34},{34,2},{3,35},{35,3},{4,36},{36... | collective-permute-start | bytes 2985992 | tf_op jit(solution)/shard_map/ppermute | solution.py:222
  96.2 1.1 pad_maximum_fusion.1
  97.3 2.4 %collective-permute-start.8 = (bf16[4,72,1728]{2,1,0:T(8,128)(2,1)S(1)}, bf16[4,72,1728]{2,1,0:T(8,128)(2,1)}, u32[]{:S(2)}, u32[]{:S(2)}) collective-permute-start(bf16[4,72,1728]{2,1,0:T(8,128)(2,1)S(1)} %pad_maximum_fusion.1), channel_id=1, source_target_pairs={{0,32},{32,0},{1,33},{33,1},{2,34},{34,2},{3,35},{35,3},{4,36},{36... | collective-permute-start | bytes 2985992 | tf_op jit(solution)/shard_map/ppermute | solution.py:223
  101.5 8.0 %all-to-all-done = bf16[16,16,1152]{2,1,0:T(8,128)(2,1)S(1)} async-done(((bf16[16,16,1152]{2,1,0:T(8,128)(2,1)}), bf16[16,16,1152]{2,1,0:T(8,128)(2,1)S(1)}, u32[]{:S(2)}, u32[]{:S(2)}) %all-to-all-start) | async-done | bytes 589856 | tf_op jit(solution)/shard_map/all_to_all | solution.py:218
  110.3 3.4 %shard_map.92.normed_ref = bf16[192,1536]{1,0:T(8,128)(2,1)} custom-call(bf16[256,1152]{1,0:T(8,128)(2,1)} %bitcast.33, s32[1,1536]{1,0:T(1,128)} %reshape.581.index_ref), custom_call_target="tpu_custom_call" | custom-call | tf_op jit(solution)/shard_map/pallas_call | solution.py:240
  113.8 7.6 %shard_map.93 = bf16[256,576]{1,0:T(8,128)(2,1)} custom-call(bf16[192,1536]{1,0:T(8,128)(2,1)} %shard_map.92.normed_ref, bf16[288,1728]{1,0:T(8,128)(2,1)} %bitcast.31, bf16[288,1728]{1,0:T(8,128)(2,1)} %bitcast.8.a8_ref, bf16[288,1728]{1,0:T(8,128)(2,1)} %bitcast.32, bf16[288,1728]{1,0:T(8,128)(2,1)} %bitcast.14.b8_ref), custom_call_target="tpu_custom_call" | custom-call | tf_op jit(solution)/shard_map/pallas_call | solution.py:241
  121.4 5.5 %all-to-all-start.1 = ((bf16[16,16,576]{2,1,0:T(8,128)(2,1)}), bf16[16,16,576]{2,1,0:T(8,128)(2,1)S(1)}, u32[]{:S(2)}, u32[]{:S(2)}) async-start(bf16[16,16,576]{2,1,0:T(8,128)(2,1)} %bitcast.37), calls=%async_computation.1 | async-start | bytes 655360 | tf_op jit(solution)/shard_map/all_to_all | solution.py:244
  129.0 12.5 %shard_map.95 = (bf16[2048,576]{1,0:T(8,128)(2,1)}, bf16[2048,576]{1,0:T(8,128)(2,1)}) custom-call(s32[1]{0:T(128)} %bitcast.20.yh_ref, bf16[8,256,1152]{2,1,0:T(8,128)(2,1)} %bitcast.27, bf16[8,256,1152]{2,1,0:T(8,128)(2,1)} %bitcast.29), custom_call_target="tpu_custom_call" | custom-call | tf_op jit(solution)/shard_map/pallas_call | solution.py:264
  142.2 14.0 %shard_map.96 = bf16[192,1152]{1,0:T(8,128)(2,1)} custom-call(s32[3,8]{1,0:T(4,128)} %select_reduce_fusion.ids_ref, bf16[192,1152]{1,0:T(8,128)(2,1)} %bitcast.36, bf16[256,576]{1,0:T(8,128)(2,1)} %bitcast.38, f32[3,512]{1,0:T(4,128)} %convert_element_type.6.live_ref, s32[1,768]{1,0:T(1,128)} %compare_select_fusion.5.cols36_ref, ...), custom_call_target="tpu_custom_call" | custom-call | tf_op jit(solution)/shard_map/pallas_call | solution.py:267
  (44 shorter events, 7.0 us)
Async XLA Ops:
  6.5 93.2 %copy-start.6 = (s32[3,1,32]{2,1,0:T(1,128)S(1)}, s32[3,1,32]{2,1,0:T(1,128)}, u32[]{:S(2)}) copy-start(s32[3,1,32]{2,1,0:T(1,128)} %param.10) | copy-start | bytes 1156
  6.5 122.4 %all-gather.5.cloned.1.call-start = ((), (), s32[]{:S(2)}) async-start(), calls=%async_computation.2 | async-start | bytes 5308416 | tf_op jit(solution)/shard_map/all_gather | solution.py:229
  8.7 120.2 %all-gather.7.cloned.1.call-start = ((), (), s32[]{:S(2)}) async-start(), calls=%async_computation.3 | async-start | bytes 5308416 | tf_op jit(solution)/shard_map/all_gather | solution.py:230
  8.8 13.9 %collective-permute-start.1 = (bf16[72,1728]{1,0:T(8,128)(2,1)}, bf16[72,1728]{1,0:T(8,128)(2,1)S(1)}, u32[]{:S(2)}, u32[]{:S(2)}) collective-permute-start(bf16[72,1728]{1,0:T(8,128)(2,1)} %param.12), channel_id=1, source_target_pairs={{0,384},{128,0},{256,128},{384,256},{1,385},{129,1},{257,129},{385... | collective-permute-start | bytes 746504 | tf_op jit(solution)/shard_map/ppermute | solution.py:197
  11.5 15.4 %collective-permute-start = (bf16[72,1728]{1,0:T(8,128)(2,1)}, bf16[72,1728]{1,0:T(8,128)(2,1)S(1)}, u32[]{:S(2)}, u32[]{:S(2)}) collective-permute-start(bf16[72,1728]{1,0:T(8,128)(2,1)} %param.12), channel_id=1, source_target_pairs={{0,128},{128,256},{256,384},{384,0},{1,129},{129,257},{257,385},{3... | collective-permute-start | bytes 746504 | tf_op jit(solution)/shard_map/ppermute | solution.py:197
  15.9 11.1 %collective-permute-start.2 = (bf16[72,1728]{1,0:T(8,128)(2,1)}, bf16[72,1728]{1,0:T(8,128)(2,1)S(1)}, u32[]{:S(2)}, u32[]{:S(2)}) collective-permute-start(bf16[72,1728]{1,0:T(8,128)(2,1)} %param.12), channel_id=1, source_target_pairs={{0,256},{128,384},{256,0},{384,128},{1,257},{129,385},{257,1},{385... | collective-permute-start | bytes 746504 | tf_op jit(solution)/shard_map/ppermute | solution.py:197
  18.0 18.8 %collective-permute-start.4 = (bf16[72,1728]{1,0:T(8,128)(2,1)}, bf16[72,1728]{1,0:T(8,128)(2,1)S(1)}, u32[]{:S(2)}, u32[]{:S(2)}) collective-permute-start(bf16[72,1728]{1,0:T(8,128)(2,1)} %param.12), channel_id=1, source_target_pairs={{0,64},{64,0},{1,65},{65,1},{2,66},{66,2},{3,67},{67,3},{4,68},{68... | collective-permute-start | bytes 746504 | tf_op jit(solution)/shard_map/ppermute | solution.py:215
  28.0 85.7 %copy-start = (bf16[4,72,1728]{2,1,0:T(8,128)(2,1)}, bf16[4,72,1728]{2,1,0:T(8,128)(2,1)S(1)}, u32[]{:S(2)}) copy-start(bf16[4,72,1728]{2,1,0:T(8,128)(2,1)S(1)} %pad_maximum_fusion) | copy-start | bytes 2985988
  36.8 29.6 %collective-permute-start.9 = (bf16[256,1152]{1,0:T(8,128)(2,1)}, bf16[256,1152]{1,0:T(8,128)(2,1)S(1)}, u32[]{:S(2)}, u32[]{:S(2)}) collective-permute-start(bf16[256,1152]{1,0:T(8,128)(2,1)} %shard_map.94), channel_id=1, source_target_pairs={{0,64},{64,0},{1,65},{65,1},{2,66},{66,2},{3,67},{67,3},{4,68},{68... | collective-permute-start | bytes 1769480 | tf_op jit(solution)/shard_map/ppermute | solution.py:228
  66.4 0.8 copy-start.4
  67.3 28.2 %collective-permute-start.7 = (bf16[72,1728]{1,0:T(8,128)(2,1)S(1)}, bf16[72,1728]{1,0:T(8,128)(2,1)S(1)}, u32[]{:S(2)}, u32[]{:S(2)}) collective-permute-start(bf16[72,1728]{1,0:T(8,128)(2,1)S(1)} %collective-permute-done.4), channel_id=1, source_target_pairs={{0,256},{128,384},{256,0},{384,128},{1,257},{129,385},{257,1},{385... | collective-permute-start | bytes 746504 | tf_op jit(solution)/shard_map/ppermute | solution.py:197
  72.3 23.2 %collective-permute-start.6 = (bf16[72,1728]{1,0:T(8,128)(2,1)S(1)}, bf16[72,1728]{1,0:T(8,128)(2,1)S(1)}, u32[]{:S(2)}, u32[]{:S(2)}) collective-permute-start(bf16[72,1728]{1,0:T(8,128)(2,1)S(1)} %collective-permute-done.4), channel_id=1, source_target_pairs={{0,384},{128,0},{256,128},{384,256},{1,385},{129,1},{257,129},{385... | collective-permute-start | bytes 746504 | tf_op jit(solution)/shard_map/ppermute | solution.py:197
  74.2 21.3 %collective-permute-start.5 = (bf16[72,1728]{1,0:T(8,128)(2,1)S(1)}, bf16[72,1728]{1,0:T(8,128)(2,1)S(1)}, u32[]{:S(2)}, u32[]{:S(2)}) collective-permute-start(bf16[72,1728]{1,0:T(8,128)(2,1)S(1)} %collective-permute-done.4), channel_id=1, source_target_pairs={{0,128},{128,256},{256,384},{384,0},{1,129},{129,257},{257,385},{3... | collective-permute-start | bytes 746504 | tf_op jit(solution)/shard_map/ppermute | solution.py:197
  81.5 28.0 %all-to-all-start = ((bf16[16,16,1152]{2,1,0:T(8,128)(2,1)}), bf16[16,16,1152]{2,1,0:T(8,128)(2,1)S(1)}, u32[]{:S(2)}, u32[]{:S(2)}) async-start(bf16[16,16,1152]{2,1,0:T(8,128)(2,1)} %bitcast.34), calls=%async_computation | async-start | bytes 1179648 | tf_op jit(solution)/shard_map/all_to_all | solution.py:218
  93.5 20.2 %collective-permute-start.3 = (bf16[4,72,1728]{2,1,0:T(8,128)(2,1)S(1)}, bf16[4,72,1728]{2,1,0:T(8,128)(2,1)}, u32[]{:S(2)}, u32[]{:S(2)}) collective-permute-start(bf16[4,72,1728]{2,1,0:T(8,128)(2,1)S(1)} %pad_maximum_fusion), channel_id=1, source_target_pairs={{0,32},{32,0},{1,33},{33,1},{2,34},{34,2},{3,35},{35,3},{4,36},{36... | collective-permute-start | bytes 2985992 | tf_op jit(solution)/shard_map/ppermute | solution.py:222
  95.5 0.7 copy-start.5
  97.3 16.5 %copy-start.1 = (bf16[4,72,1728]{2,1,0:T(8,128)(2,1)}, bf16[4,72,1728]{2,1,0:T(8,128)(2,1)S(1)}, u32[]{:S(2)}) copy-start(bf16[4,72,1728]{2,1,0:T(8,128)(2,1)S(1)} %pad_maximum_fusion.1) | copy-start | bytes 2985988
  97.3 16.5 %collective-permute-start.8 = (bf16[4,72,1728]{2,1,0:T(8,128)(2,1)S(1)}, bf16[4,72,1728]{2,1,0:T(8,128)(2,1)}, u32[]{:S(2)}, u32[]{:S(2)}) collective-permute-start(bf16[4,72,1728]{2,1,0:T(8,128)(2,1)S(1)} %pad_maximum_fusion.1), channel_id=1, source_target_pairs={{0,32},{32,0},{1,33},{33,1},{2,34},{34,2},{3,35},{35,3},{4,36},{36... | collective-permute-start | bytes 2985992 | tf_op jit(solution)/shard_map/ppermute | solution.py:223
  109.5 0.8 copy-start.2
  121.4 20.1 %all-to-all-start.1 = ((bf16[16,16,576]{2,1,0:T(8,128)(2,1)}), bf16[16,16,576]{2,1,0:T(8,128)(2,1)S(1)}, u32[]{:S(2)}, u32[]{:S(2)}) async-start(bf16[16,16,576]{2,1,0:T(8,128)(2,1)} %bitcast.37), calls=%async_computation.1 | async-start | bytes 655360 | tf_op jit(solution)/shard_map/all_to_all | solution.py:244
  141.5 0.7 copy-start.3
Sparse Core Ops, SparseCore 0:
  9.5 41.7 all-gather.4
  67.4 40.7 all-gather.6

commit v2 on v1

v2 whole, which is shorter than its diff:
```python
import functools

import jax
import jax.numpy as jnp
from jax import lax
from jax.experimental import pallas as pl
from jax.experimental.pallas import tpu as pltpu
from jax.sharding import Mesh
from jax.sharding import PartitionSpec as P

HEADS = 8
HEAD = 72
INNER = 576
HALF = 288
WIDTH = 1152
CHANNELS = 512
EPS = 1e-06
SCALE = HEAD ** (-0.5)
BF = jnp.bfloat16
F32 = jnp.float32

PACK = 896
REST, SLAB, SHARE = 144, 128, 272


def mm(a, b):
    return lax.dot_general(a, b, (((1,), (0,)), ((), ())), preferred_element_type=F32)


def mm_nt(a, b):
    return lax.dot_general(a, b, (((1,), (1,)), ((), ())), preferred_element_type=F32)


def iota(shape, dim):
    return lax.broadcasted_iota(jnp.int32, shape, dim)


def onehot(hit):
    return jnp.where(hit, 1.0, 0.0).astype(BF)


def split_mm(a, b):
    high = a.astype(BF)
    low = (a - high.astype(F32)).astype(BF)
    return mm(high, b) + mm(low, b)


def head_normalize(values):
    width = values.shape[1]
    gather = onehot(iota((width, 128), 0) // HEAD == iota((width, 128), 1))
    spread = onehot(iota((128, width), 1) // HEAD == iota((128, width), 0))
    mean = split_mm(values * values, gather) * (1.0 / HEAD)
    return values * split_mm(lax.rsqrt(mean + EPS), spread)


def rms_rows(values):
    return values * lax.rsqrt(jnp.mean(values * values, axis=-1, keepdims=True) + EPS)


def head_masked(rows):
    head = iota(rows.shape, 1) // HEAD
    return jnp.concatenate([jnp.where(head == h, rows, 0.0).astype(BF) for h in range(4)], axis=0)


def head_merged(rows, count):
    head = iota((count, HALF), 1) // HEAD
    total = rows[:count]
    for h in range(1, 4):
        total = jnp.where(head == h, rows[h * count:(h + 1) * count], total)
    return total.astype(BF)


def first_kernel(l_ref, qkv_ref, occ_ref, kv_ref, lat_ref, cq_ref, out_ref, co_ref,
                 packed_ref, own_ref, share_ref, sent_ref):
    share_ref[...] = jnp.zeros(share_ref.shape, BF)
    rest = jnp.concatenate([out_ref[...], co_ref[...]], axis=0)
    share_ref[0:72, :] = rest[:, 0:PACK]
    share_ref[72:144, 0:256] = rest[:, PACK:]
    share_ref[72:144, 256:256 + INNER] = cq_ref[...]
    share_ref[REST:, 0:CHANNELS] = occ_ref[...]
    for q in range(4):
        at = slice(REST + 32 * q, REST + 32 * q + 32)
        share_ref[at, CHANNELS:CHANNELS + HALF] = kv_ref[:, q * HALF:(q + 1) * HALF]
    packed_ref[0:SHARE, :] = share_ref[...]
    packed_ref[SHARE:, 3 * HALF:] = jnp.zeros((72, PACK - 3 * HALF), BF)
    first = l_ref[0] == 0
    for n in range(3):
        low = qkv_ref[:, n * INNER:n * INNER + HALF]
        high = qkv_ref[:, n * INNER + HALF:(n + 1) * INNER]
        own_ref[:, n * HALF:(n + 1) * HALF] = jnp.where(first, low, high)
        packed_ref[SHARE:, n * HALF:(n + 1) * HALF] = jnp.where(first, high, low)
    to, src = iota((192, 192), 0), iota((192, 192), 1)
    pick = onehot(src == (to // 8) % 3 * 64 + to // 24 * 8 + to % 8)
    rows = mm(pick, lat_ref[...]).astype(BF)
    sent_ref[0:192, :] = rows
    sent_ref[192:384, :] = rows


def prep_kernel(rows_ref, index_ref, own_ref, swapped_ref, normed_ref, qkv_ref, share_ref):
    share_ref[...] = swapped_ref[0:SHARE, :]
    qkv_ref[0] = own_ref[...]
    qkv_ref[1] = swapped_ref[SHARE:, 0:3 * HALF]
    normed = rms_rows(rows_ref[...].astype(F32)).astype(BF)
    for at in range(0, 1280, 256):
        spread = onehot(iota((WIDTH, 256), 0) == index_ref[:, at:at + 256])
        normed_ref[:, at:at + 256] = mm(normed, spread).astype(BF)


def temporal_kernel(normed_ref, own_ref, other_ref, mixed_ref):
    projected = mm(normed_ref[:, 0:INNER], own_ref[...]) + mm(
        normed_ref[:, 640:640 + INNER], other_ref[...]
    )
    both = head_normalize(projected[:, :INNER])
    query = both[:, :HALF]
    key = both[:, HALF:].astype(BF)
    value = projected[:, INNER:].astype(BF)
    live = iota((512, 128), 0) % 8 == iota((512, 128), 1) % 8
    for view in range(3):
        rows = slice(view * 128, view * 128 + 128)
        scores = mm_nt(head_masked(query[rows]), key[rows]) * SCALE
        exponent = jnp.where(live, jnp.exp(scores), 0.0)
        weights = (exponent * (1.0 / jnp.sum(exponent, axis=-1, keepdims=True))).astype(BF)
        mixed_ref[rows, :] = head_merged(mm(weights, value[rows]), 128)


def slab_kernel(index_ref, a_ref, b_ref, slab_ref, rows_ref, held_ref, in_sem, out_sem):
    arrivals = []
    for n in range(16):
        at = pl.ds(n % 8 * SHARE + REST, SLAB)
        arrivals.append(
            pltpu.make_async_copy((a_ref, b_ref)[n // 8].at[at], rows_ref.at[pl.ds(n * SLAB, SLAB)], in_sem.at[n])
        )
        arrivals[-1].start()
    order = onehot(iota((CHANNELS, CHANNELS), 0) == index_ref[...])
    gather = onehot(iota((640, 128), 0) // HEAD == iota((640, 128), 1)) * onehot(iota((640, 128), 1) < HEADS)
    spread = onehot(jnp.minimum(iota((128, WIDTH), 1) // HEAD, HEADS) == iota((128, WIDTH), 0))
    for copy in arrivals:
        copy.wait()
    quarters = []
    for q in range(4):
        parts = [rows_ref[n * SLAB + 32 * q:n * SLAB + 32 * q + 32, CHANNELS:CHANNELS + HALF] for n in range(16)]
        quarters.append(jnp.concatenate(parts, axis=0))
    weight = mm(order, jnp.concatenate(quarters, axis=1)).astype(BF)
    copies = []
    for part in range(8):
        rows = pl.ds(part * 256, 256)
        projected = mm(rows_ref[rows, 0:CHANNELS], weight)
        mean = split_mm(projected[:, :640] * projected[:, :640], gather) * (1.0 / HEAD)
        factor = jnp.where(iota((256, 128), 1) < HEADS, lax.rsqrt(mean + EPS), 1.0)
        held_ref[rows, :] = (projected * split_mm(factor, spread)).astype(BF)
        copies.append(pltpu.make_async_copy(held_ref.at[rows], slab_ref.at[rows], out_sem.at[part]))
        copies[-1].start()
    for copy in copies:
        copy.wait()


def cross_kernel(ids_ref, lat_ref, mixed_ref, live_ref, index72_ref, index36_ref, a_ref, b_ref, slab_ref,
                 result_ref, a_held, b_held, picked_ref, out_ref, co_ref, cq_ref, sem):
    weights = []
    for n in range(16):
        at = pl.ds(n % 8 * SHARE, REST)
        held = (a_held, b_held)[n // 8].at[pl.ds(n % 8 * REST, REST)]
        weights.append(pltpu.make_async_copy((a_ref, b_ref)[n // 8].at[at], held, sem.at[24 + n]))
        weights[-1].start()
    blocks = []
    for n in range(24):
        block = pl.ds(pl.multiple_of(ids_ref[n // 8, n % 8] * 64, 64), 64)
        blocks.append(pltpu.make_async_copy(slab_ref.at[block], picked_ref.at[pl.ds(n * 64, 64)], sem.at[n]))
        blocks[-1].start()

    to, src = iota((192, 192), 0), iota((192, 192), 1)
    pick = onehot(src == (to % 64) // 8 * 24 + to // 64 * 8 + to % 8)
    spread36 = onehot(iota((INNER, INNER), 0) == index36_ref[...])
    halves = [mm(pick, mixed_ref[at:at + 192, :]).astype(BF) for at in (0, 192)]
    mixed = mm(halves[0], spread36[:HALF]) + mm(halves[1], spread36[HALF:])
    spread72 = onehot(iota((WIDTH, WIDTH), 0) == index72_ref[...])
    for side, ref in enumerate((a_held, b_held)):
        for j in range(8):
            weights[side * 8 + j].wait()
            to = slice(side * HALF + j * 36, side * HALF + j * 36 + 36)
            at = j * 144
            out_ref[to, 0:PACK] = ref[at:at + 36, :]
            co_ref[to, 0:PACK] = ref[at + 36:at + 72, :]
            out_ref[to, PACK:] = ref[at + 72:at + 108, 0:256]
            co_ref[to, PACK:] = ref[at + 108:at + 144, 0:256]
            cq_ref[side * INNER + j * 72:side * INNER + j * 72 + 72, :] = ref[at + 72:at + 144, 256:256 + INNER]
    hidden = (lat_ref[...].astype(F32) + mm(mixed.astype(BF), out_ref[...])).astype(BF)
    normed = rms_rows(hidden.astype(F32)).astype(BF)
    query = head_normalize(mm(mm(normed, spread72).astype(BF), cq_ref[...]))
    query = jnp.concatenate([query, jnp.zeros((192, 64), F32)], axis=1)
    head = iota((64, 640), 1) // HEAD
    value_head = (iota((64, 640), 1) - 64 + HEAD) // HEAD - 1
    crossed = []
    for tile in range(3):
        for copy in blocks[tile * 8:tile * 8 + 8]:
            copy.wait()
        rows = query[tile * 64:tile * 64 + 64]
        masked = jnp.concatenate([jnp.where(head == h, rows, 0.0).astype(BF) for h in range(HEADS)], axis=0)
        keys = slice(tile * 512, tile * 512 + 512)
        scores = mm_nt(masked, picked_ref[keys, 0:640]) * SCALE
        exponent = jnp.exp(scores) * live_ref[tile:tile + 1, :]
        weights = (exponent * (1.0 / jnp.sum(exponent, axis=-1, keepdims=True))).astype(BF)
        mixed = mm(weights, picked_ref[keys, 512:WIDTH])
        total = mixed[:64]
        for h in range(1, HEADS):
            total = jnp.where(value_head == h, mixed[h * 64:h * 64 + 64], total)
        crossed.append(total)
    crossed = jnp.concatenate(crossed, axis=0)[:, 64:].astype(BF)
    columns = mm(crossed, spread36).astype(BF)
    result_ref[...] = (hidden.astype(F32) + mm(columns, co_ref[...])).astype(BF)


def call(kernel, shapes, count, scalars=(), hbm=(), out_hbm=False, scratch=(), us=1, vmem=60):
    memory = [pltpu.SMEM if n in scalars else pl.ANY if n in hbm else pltpu.VMEM for n in range(count)]
    out_memory = pl.ANY if out_hbm else pltpu.VMEM
    return pl.pallas_call(
        kernel,
        out_shape=shapes,
        in_specs=[pl.BlockSpec(memory_space=m) for m in memory],
        out_specs=jax.tree.map(lambda _: pl.BlockSpec(memory_space=out_memory), shapes),
        scratch_shapes=scratch,
        compiler_params=pltpu.CompilerParams(vmem_limit_bytes=vmem * 1024 * 1024),
        cost_estimate=pl.CostEstimate(flops=us * 1150000000, bytes_accessed=us * 1000000, transcendentals=0),
    )


def after(values, *others):
    count = len(values)
    return lax.optimization_barrier(tuple(values) + others)[:count]


SWAP = [(0, 1), (1, 0)]
STEPS = (0, 1, 3, 2)


def along_x(block):
    return [block] + [lax.ppermute(block, "x", [(i, (i + s) % 4) for i in range(4)]) for s in STEPS[1:]]


def across_core(blocks):
    stacked = jnp.stack(blocks)
    return stacked, lax.ppermute(stacked, "c", SWAP)


def places(device, sides, rows, pad):
    place = jnp.arange(sides * pad, dtype=jnp.int32)
    side, row = place // pad, place % pad
    x, yh, c = device(side, row // rows)
    start = ((x * 2 + yh) * 2 + c) * rows
    return jnp.where(row < 16 // sides * rows, start + row % rows, -1).reshape(1, sides * pad)


def shards(latents, block_mask, occupancy, temporal_qkv, temporal_out, cross_query, cross_keyval, cross_out):
    x, yh, c, l = (lax.axis_index(name) for name in ("x", "yh", "c", "l"))
    shape = jax.ShapeDtypeStruct
    lat = latents.reshape(192, WIDTH)

    def by_step(side, j):
        return (x - jnp.array(STEPS, jnp.int32)[jnp.minimum(j // 2, 3)] + 4) % 4, yh ^ (j % 2), c ^ side

    def by_x_core(side, j):
        return j // 2, yh ^ side, j % 2

    packed, qkv, share, sent = call(
        first_kernel,
        (shape((SHARE + 72, PACK), BF), shape((72, 3 * HALF), BF), shape((SHARE, PACK), BF), shape((384, WIDTH), BF)),
        8, scalars=(0,), us=3,
    )(
        l.reshape(1).astype(jnp.int32), temporal_qkv, occupancy.reshape(128, CHANNELS), cross_keyval,
        lat, cross_query, temporal_out, cross_out,
    )
    swapped = lax.ppermute(packed, ("yh", "g", "l"), [(y, 7 - y) for y in range(8)])
    share_a = lax.all_gather(share, ("x", "c"), axis=0, tiled=True)
    time_rows = lax.all_to_all(
        sent.reshape(16, 24, WIDTH), ("l", "z"), split_axis=0, concat_axis=0, tiled=True
    ).reshape(384, WIDTH)
    normed, qkv_both, share_swapped = call(
        prep_kernel,
        (shape((384, 1280), BF), shape((2, 72, 3 * HALF), BF), shape((SHARE, PACK), BF)),
        4, us=3, vmem=24,
    )(time_rows, places(by_step, 2, 72, 640), qkv, swapped)
    share_b = lax.all_gather(share_swapped, ("x", "c"), axis=0, tiled=True)
    qkv_own, qkv_other = across_core(along_x(qkv_both))
    mixed = call(temporal_kernel, shape((384, HALF), BF), 3, us=5, vmem=24)(
        normed, qkv_own.reshape(INNER, 3 * HALF), qkv_other.reshape(INNER, 3 * HALF)
    )
    mixed_home = lax.all_to_all(
        mixed.reshape(16, 24, HALF), ("l", "z"), split_axis=0, concat_axis=0, tiled=True
    ).reshape(384, HALF)

    mask = block_mask[:, 0, :]
    rank = jnp.cumsum(mask, axis=1) - 1
    block = jnp.arange(32, dtype=jnp.int32)
    vox, half = block // 2, block % 2
    stored = ((vox // 2 % 2 ^ yh) * 8 + vox // 4 * 2 + vox % 2) * 2 + half
    chosen = (rank[:, :, None] == jnp.arange(8, dtype=jnp.int32)) & (mask[:, :, None] > 0)
    ids = jnp.sum(jnp.where(chosen, stored[None, :, None], 0), axis=1).astype(jnp.int32)
    live = jnp.repeat(jnp.any(chosen, axis=1), 64, axis=1).astype(F32)

    keys_values = call(
        slab_kernel, shape((2048, WIDTH), BF), 3, hbm=(1, 2), out_hbm=True, us=10,
        scratch=[
            pltpu.VMEM((2048, PACK), BF),
            pltpu.VMEM((2048, WIDTH), BF),
            pltpu.SemaphoreType.DMA((16,)),
            pltpu.SemaphoreType.DMA((8,)),
        ],
    )(places(by_x_core, 2, 32, 256), share_a, share_b)
    result = call(
        cross_kernel, shape((192, WIDTH), BF), 9, scalars=(0,), hbm=(6, 7, 8), us=10,
        scratch=[
            pltpu.VMEM((WIDTH, PACK), BF),
            pltpu.VMEM((WIDTH, PACK), BF),
            pltpu.VMEM((24 * 64, WIDTH), BF),
            pltpu.VMEM((INNER, WIDTH), BF),
            pltpu.VMEM((INNER, WIDTH), BF),
            pltpu.VMEM((WIDTH, INNER), BF),
            pltpu.SemaphoreType.DMA((40,)),
        ],
    )(
        ids, lat, mixed_home, live, places(by_x_core, 2, 72, INNER), places(by_x_core, 2, 36, HALF),
        share_a, share_b, keys_values,
    )
    return result.reshape(latents.shape)


def solution(mesh):
    split = Mesh(mesh.devices.reshape(4, 2, 2, 2, 2, 8), ("x", "yh", "c", "g", "l", "z"))
    vox, vf = ("x", "yh", "c"), ("g", "l", "z")
    return jax.shard_map(
        shards,
        mesh=split,
        in_specs=(
            P(vf, vox, None),
            P(vf, vox, None),
            P(vox, None, None),
            P(vox, None),
            P(vox, None),
            P(vox, None),
            P(vox, None),
            P(vox, None),
        ),
        out_specs=P(vf, vox, None),
        check_vma=False,
    )
```

time: 164 us -> 126 us (0.77)
  the two profiles are of different devices: /device:TPU:62 before, /device:TPU:1 now
where the time goes in v2:
time: 126 us
  starting transfers between devices  39.3 us (31%)
  Pallas kernels  33.8 us (27%)
  waiting for transfers between devices  33.5 us (27%)
  between operations  13.6 us (11%)
  other arithmetic  3.46 us (3%)
  local copies, waits for them, and re-layouts  2.37 us (2%)
    ppermute x1, waiting for transfers between devices, shards(): lax.ppermute(packed, ('yh', 'g', 'l'), [(y, 7 - y) for y in range(8)])  26.2 us
    pallas_call x1, Pallas kernels, shards(): call(slab_kernel, shape((2048, WIDTH), BF), 3, hbm=(1, 2), out_hbm=True,...  12.3 us
    all_to_all x1, starting transfers between devices, shards(): lax.all_to_all(sent.reshape(16, 24, WIDTH), ('l', 'z'), split_axis=0, con...  12 us
    pallas_call x1, Pallas kernels, shards(): call(cross_kernel, shape((192, WIDTH), BF), 9, scalars=(0,), hbm=(6, 7, 8...  11.8 us
    ppermute x3, starting transfers between devices, along_x(): lax.ppermute(block, 'x', [(i, (i + s) % 4) for i in range(4)])  9.94 us
    all_to_all x1, starting transfers between devices, shards(): lax.all_to_all(mixed.reshape(16, 24, HALF), ('l', 'z'), split_axis=0, con...  6.65 us
    ppermute x3, waiting for transfers between devices, along_x(): lax.ppermute(block, 'x', [(i, (i + s) % 4) for i in range(4)])  5.52 us
    ppermute x1, starting transfers between devices, across_core(): return (stacked, lax.ppermute(stacked, 'c', SWAP))  5.49 us
  transfers between devices with their start and end apart: 9, of which 4 were waited for; matrix products, arithmetic and copies ran while one was open for 3% of the time, Pallas kernels for 15%

profile of v2, /device:TPU:1, one launch (start us, length us, event | category | flops | bytes accessed | tf_op | source)
XLA Modules:
  0.0 126.0 jit_solution(72708299335212406)
XLA Ops:
  6.5 3.1 %shard_map.91 = (bf16[344,896]{1,0:T(8,128)(2,1)}, bf16[72,864]{1,0:T(8,128)(2,1)}, bf16[272,896]{1,0:T(8,128)(2,1)}, bf16[384,1152]{1,0:T(8,128)(2,1)}) custom-call(s32[1]{0:T(128)} %bitcast.1.l_ref, bf16[72,1728]{1,0:T(8,128)(2,1)} %qkv_ref.1, bf16[128,512]{1,0:T(8,128)(2,1)} %bitcast.37, bf16[32,1152]{1,0:T(8,128)(2,1)} %kv_ref.1, ...), custom_call_target="tpu_custom_call" | custom-call | flops 3449999872 | bytes 3000000 | tf_op jit(solution)/shard_map/pallas_call | solution.py:264
  9.7 12.0 %all-to-all-start = ((bf16[16,24,1152]{2,1,0:T(8,128)(2,1)}), bf16[16,24,1152]{2,1,0:T(8,128)(2,1)S(1)}, u32[]{:S(2)}, u32[]{:S(2)}) async-start(bf16[16,24,1152]{2,1,0:T(8,128)(2,1)} %bitcast.29), calls=%async_computation | async-start | bytes 1769472 | tf_op jit(solution)/shard_map/all_to_all | solution.py:274
  21.8 5.2 %collective-permute-start = (bf16[344,896]{1,0:T(8,128)(2,1)}, bf16[344,896]{1,0:T(8,128)(2,1)S(1)}, u32[]{:S(2)}, u32[]{:S(2)}) collective-permute-start(bf16[344,896]{1,0:T(8,128)(2,1)} %get-tuple-element.14), channel_id=1, source_target_pairs={{0,88},{8,80},{16,72},{24,64},{64,24},{72,16},{80,8},{88,0},{1,89}... | collective-permute-start | bytes 1849352 | tf_op jit(solution)/shard_map/ppermute | solution.py:272
  27.1 26.2 %collective-permute-done.swapped_ref = bf16[344,896]{1,0:T(8,128)(2,1)S(1)} collective-permute-done((bf16[344,896]{1,0:T(8,128)(2,1)}, bf16[344,896]{1,0:T(8,128)(2,1)S(1)}, u32[]{:S(2)}, u32[]{:S(2)}) %collective-permute-start) | collective-permute-done | bytes 616480 | tf_op jit(solution)/shard_map/ppermute | solution.py:272
  53.3 0.9 copy-done
  54.2 2.4 %shard_map.92 = (bf16[384,1280]{1,0:T(8,128)(2,1)S(1)}, bf16[2,72,864]{2,1,0:T(8,128)(2,1)S(1)}, bf16[272,896]{1,0:T(8,128)(2,1)}) custom-call(bf16[384,1152]{1,0:T(8,128)(2,1)S(1)} %bitcast.26, s32[1,1280]{1,0:T(1,128)S(1)} %compare_select_fusion.8.index_ref, bf16[72,864]{1,0:T(8,128)(2,1)S(1)} %copy-done, bf16[344,896]{1,0:T(8,128)(2,1)S(1)} %collective-permute-done.swapped_ref), custom_call_target="tpu_custom_call" | custom-call | flops 3449999872 | bytes 3000000 | tf_op jit(solution)/shard_map/pallas_call | solution.py:277
  56.7 4.7 %collective-permute-start.3 = (bf16[2,72,864]{2,1,0:T(8,128)(2,1)S(1)}, bf16[2,72,864]{2,1,0:T(8,128)(2,1)S(1)}, u32[]{:S(2)}, u32[]{:S(2)}) collective-permute-start(bf16[2,72,864]{2,1,0:T(8,128)(2,1)S(1)} %get-tuple-element.16), channel_id=1, source_target_pairs={{0,256},{128,384},{256,0},{384,128},{1,257},{129,385},{257,1},{385... | collective-permute-start | bytes 746504 | tf_op jit(solution)/shard_map/ppermute | solution.py:237
  61.3 2.8 %collective-permute-start.2 = (bf16[2,72,864]{2,1,0:T(8,128)(2,1)S(1)}, bf16[2,72,864]{2,1,0:T(8,128)(2,1)S(1)}, u32[]{:S(2)}, u32[]{:S(2)}) collective-permute-start(bf16[2,72,864]{2,1,0:T(8,128)(2,1)S(1)} %get-tuple-element.16), channel_id=1, source_target_pairs={{0,384},{128,0},{256,128},{384,256},{1,385},{129,1},{257,129},{385... | collective-permute-start | bytes 746504 | tf_op jit(solution)/shard_map/ppermute | solution.py:237
  64.1 2.5 %collective-permute-start.1 = (bf16[2,72,864]{2,1,0:T(8,128)(2,1)S(1)}, bf16[2,72,864]{2,1,0:T(8,128)(2,1)S(1)}, u32[]{:S(2)}, u32[]{:S(2)}) collective-permute-start(bf16[2,72,864]{2,1,0:T(8,128)(2,1)S(1)} %get-tuple-element.16), channel_id=1, source_target_pairs={{0,128},{128,256},{256,384},{384,0},{1,129},{129,257},{257,385},{3... | collective-permute-start | bytes 746504 | tf_op jit(solution)/shard_map/ppermute | solution.py:237
  66.6 0.2 reduce_window_sum.14
  66.8 4.8 %collective-permute-done.2 = bf16[2,72,864]{2,1,0:T(8,128)(2,1)S(1)} collective-permute-done((bf16[2,72,864]{2,1,0:T(8,128)(2,1)S(1)}, bf16[2,72,864]{2,1,0:T(8,128)(2,1)S(1)}, u32[]{:S(2)}, u32[]{:S(2)}) %collective-permute-start.2) | collective-permute-done | bytes 248864 | tf_op jit(solution)/shard_map/ppermute | solution.py:237
  71.7 0.7 collective-permute-done.1
  72.6 5.5 %collective-permute-start.4 = (bf16[4,2,72,864]{3,2,1,0:T(8,128)(2,1)S(1)}, bf16[4,2,72,864]{3,2,1,0:T(8,128)(2,1)S(1)}, u32[]{:S(2)}, u32[]{:S(2)}) collective-permute-start(bf16[4,2,72,864]{3,2,1,0:T(8,128)(2,1)S(1)} %pad_maximum_fusion), channel_id=1, source_target_pairs={{0,32},{32,0},{1,33},{33,1},{2,34},{34,2},{3,35},{35,3},{4,36},{36... | collective-permute-start | bytes 2985992 | tf_op jit(solution)/shard_map/ppermute | solution.py:242
  78.3 0.7 convert_element_type.6.live_ref
  79.0 0.6 compare_select_fusion.17.index_ref
  79.6 0.7 compare_select_fusion.13.index36_ref
  80.3 0.7 select_reduce_fusion.ids_ref
  81.0 0.7 compare_select_fusion.9.index72_ref
  81.7 4.2 %shard_map.93 = bf16[384,288]{1,0:T(8,128)(2,1)} custom-call(bf16[384,1280]{1,0:T(8,128)(2,1)S(1)} %get-tuple-element.15.normed_ref, bf16[576,864]{1,0:T(8,128)(2,1)S(1)} %bitcast.25, bf16[576,864]{1,0:T(8,128)(2,1)S(1)} %bitcast.28), custom_call_target="tpu_custom_call" | custom-call | flops 5750000128 | bytes 5000000 | tf_op jit(solution)/shard_map/pallas_call | solution.py:284
  85.9 6.7 %all-to-all-start.1 = ((bf16[16,24,288]{2,1,0:T(8,128)(2,1)}), bf16[16,24,288]{2,1,0:T(8,128)(2,1)S(1)}, u32[]{:S(2)}, u32[]{:S(2)}) async-start(bf16[16,24,288]{2,1,0:T(8,128)(2,1)} %bitcast.12), calls=%async_computation.1 | async-start | bytes 589824 | tf_op jit(solution)/shard_map/all_to_all | solution.py:287
  92.6 1.7 %all-gather.5.cloned.1.call-done.b_ref = bf16[2176,896]{1,0:T(8,128)(2,1)} async-done(((bf16[272,896]{1,0:T(8,128)(2,1)}), bf16[2176,896]{1,0:T(8,128)(2,1)}) %all-gather.5.cloned.1.call-update) | async-done | bytes 3899408 | tf_op jit(solution)/shard_map/all_gather | solution.py:282
  94.3 12.3 %shard_map.94.slab_ref = bf16[2048,1152]{1,0:T(8,128)(2,1)} custom-call(s32[1,512]{1,0:T(1,128)} %compare_select_fusion.17.index_ref, bf16[2176,896]{1,0:T(8,128)(2,1)} %all-gather.3.cloned.1.call-done.a_ref, bf16[2176,896]{1,0:T(8,128)(2,1)} %all-gather.5.cloned.1.call-done.b_ref), custom_call_target="tpu_custom_call" | custom-call | flops 11500000256 | bytes 10000000 | tf_op jit(solution)/shard_map/pallas_call | solution.py:300
  106.6 0.7 copy-done.1
  107.3 11.8 %shard_map.95 = bf16[192,1152]{1,0:T(8,128)(2,1)} custom-call(s32[3,8]{1,0:T(4,128)} %select_reduce_fusion.ids_ref, bf16[192,1152]{1,0:T(8,128)(2,1)} %bitcast.36, bf16[384,288]{1,0:T(8,128)(2,1)} %bitcast.30, f32[3,512]{1,0:T(4,128)} %convert_element_type.6.live_ref, s32[1,1152]{1,0:T(1,128)} %compare_select_fusion.9.index72_ref, ...), custom_call_target="tpu_custom_call" | custom-call | flops 11500000256 | bytes 10000000 | tf_op jit(solution)/shard_map/pallas_call | solution.py:309
  (22 shorter events, 0.7 us)
Async XLA Ops:
  6.5 86.1 %all-gather.3.cloned.1.call-start = ((), (), s32[]{:S(2)}) async-start(), calls=%async_computation.2 | async-start | bytes 4386816 | tf_op jit(solution)/shard_map/all_gather | solution.py:273
  9.7 43.6 %all-to-all-start = ((bf16[16,24,1152]{2,1,0:T(8,128)(2,1)}), bf16[16,24,1152]{2,1,0:T(8,128)(2,1)S(1)}, u32[]{:S(2)}, u32[]{:S(2)}) async-start(bf16[16,24,1152]{2,1,0:T(8,128)(2,1)} %bitcast.29), calls=%async_computation | async-start | bytes 1769472 | tf_op jit(solution)/shard_map/all_to_all | solution.py:274
  21.7 72.6 %all-gather.5.cloned.1.call-start = ((), (), s32[]{:S(2)}) async-start(), calls=%async_computation.3 | async-start | bytes 4386816 | tf_op jit(solution)/shard_map/all_gather | solution.py:282
  21.8 31.6 %collective-permute-start = (bf16[344,896]{1,0:T(8,128)(2,1)}, bf16[344,896]{1,0:T(8,128)(2,1)S(1)}, u32[]{:S(2)}, u32[]{:S(2)}) collective-permute-start(bf16[344,896]{1,0:T(8,128)(2,1)} %get-tuple-element.14), channel_id=1, source_target_pairs={{0,88},{8,80},{16,72},{24,64},{64,24},{72,16},{80,8},{88,0},{1,89}... | collective-permute-start | bytes 1849352 | tf_op jit(solution)/shard_map/ppermute | solution.py:272
  53.3 0.9 copy-start
  54.2 12.4 %copy-start.2 = (s32[3,1,32]{2,1,0:T(1,128)S(1)}, s32[3,1,32]{2,1,0:T(1,128)}, u32[]{:S(2)}) copy-start(s32[3,1,32]{2,1,0:T(1,128)} %param.10) | copy-start | bytes 1156
  56.7 10.2 %collective-permute-start.3 = (bf16[2,72,864]{2,1,0:T(8,128)(2,1)S(1)}, bf16[2,72,864]{2,1,0:T(8,128)(2,1)S(1)}, u32[]{:S(2)}, u32[]{:S(2)}) collective-permute-start(bf16[2,72,864]{2,1,0:T(8,128)(2,1)S(1)} %get-tuple-element.16), channel_id=1, source_target_pairs={{0,256},{128,384},{256,0},{384,128},{1,257},{129,385},{257,1},{385... | collective-permute-start | bytes 746504 | tf_op jit(solution)/shard_map/ppermute | solution.py:237
  61.3 10.4 %collective-permute-start.2 = (bf16[2,72,864]{2,1,0:T(8,128)(2,1)S(1)}, bf16[2,72,864]{2,1,0:T(8,128)(2,1)S(1)}, u32[]{:S(2)}, u32[]{:S(2)}) collective-permute-start(bf16[2,72,864]{2,1,0:T(8,128)(2,1)S(1)} %get-tuple-element.16), channel_id=1, source_target_pairs={{0,384},{128,0},{256,128},{384,256},{1,385},{129,1},{257,129},{385... | collective-permute-start | bytes 746504 | tf_op jit(solution)/shard_map/ppermute | solution.py:237
  64.1 8.3 %collective-permute-start.1 = (bf16[2,72,864]{2,1,0:T(8,128)(2,1)S(1)}, bf16[2,72,864]{2,1,0:T(8,128)(2,1)S(1)}, u32[]{:S(2)}, u32[]{:S(2)}) collective-permute-start(bf16[2,72,864]{2,1,0:T(8,128)(2,1)S(1)} %get-tuple-element.16), channel_id=1, source_target_pairs={{0,128},{128,256},{256,384},{384,0},{1,129},{129,257},{257,385},{3... | collective-permute-start | bytes 746504 | tf_op jit(solution)/shard_map/ppermute | solution.py:237
  72.6 9.2 %collective-permute-start.4 = (bf16[4,2,72,864]{3,2,1,0:T(8,128)(2,1)S(1)}, bf16[4,2,72,864]{3,2,1,0:T(8,128)(2,1)S(1)}, u32[]{:S(2)}, u32[]{:S(2)}) collective-permute-start(bf16[4,2,72,864]{3,2,1,0:T(8,128)(2,1)S(1)} %pad_maximum_fusion), channel_id=1, source_target_pairs={{0,32},{32,0},{1,33},{33,1},{2,34},{34,2},{3,35},{35,3},{4,36},{36... | collective-permute-start | bytes 2985992 | tf_op jit(solution)/shard_map/ppermute | solution.py:242
  85.9 20.6 %all-to-all-start.1 = ((bf16[16,24,288]{2,1,0:T(8,128)(2,1)}), bf16[16,24,288]{2,1,0:T(8,128)(2,1)S(1)}, u32[]{:S(2)}, u32[]{:S(2)}) async-start(bf16[16,24,288]{2,1,0:T(8,128)(2,1)} %bitcast.12), calls=%async_computation.1 | async-start | bytes 589824 | tf_op jit(solution)/shard_map/all_to_all | solution.py:287
  106.6 0.7 copy-start.1
Sparse Core Ops, SparseCore 0:
  9.8 42.0 all-gather.2
  56.8 37.4 all-gather.4

commit v3 on v2

v3 whole, which is shorter than its diff:
```python
import functools

import jax
import jax.numpy as jnp
from jax import lax
from jax.experimental import pallas as pl
from jax.experimental.pallas import tpu as pltpu
from jax.sharding import Mesh
from jax.sharding import PartitionSpec as P

HEADS = 8
HEAD = 72
INNER = 576
HALF = 288
WIDTH = 1152
CHANNELS = 512
EPS = 1e-06
SCALE = HEAD ** (-0.5)
BF = jnp.bfloat16
F32 = jnp.float32

PACK = 896
REST, SLAB, SHARE = 144, 128, 272


def mm(a, b):
    return lax.dot_general(a, b, (((1,), (0,)), ((), ())), preferred_element_type=F32)


def mm_nt(a, b):
    return lax.dot_general(a, b, (((1,), (1,)), ((), ())), preferred_element_type=F32)


def iota(shape, dim):
    return lax.broadcasted_iota(jnp.int32, shape, dim)


def onehot(hit):
    return jnp.where(hit, 1.0, 0.0).astype(BF)


def head_sums(width, count):
    row = iota((width, 128), 0) // HEAD
    return onehot((row == iota((width, 128), 1)) & (row < count))


def head_spread(width, count):
    return onehot(iota((256, width), 0) % 128 == jnp.minimum(iota((256, width), 1) // HEAD, count))


def head_factors(values, sums, count):
    squares = values * values
    high = squares.astype(BF)
    low = (squares - high.astype(F32)).astype(BF)
    mean = (mm(high, sums) + mm(low, sums)) * (1.0 / HEAD)
    factor = jnp.where(iota(mean.shape, 1) < count, lax.rsqrt(mean + EPS), 1.0)
    high = factor.astype(BF)
    return jnp.concatenate([high, (factor - high.astype(F32)).astype(BF)], axis=1)


def head_normalize(values):
    width = values.shape[1]
    count = width // HEAD
    return values * mm(head_factors(values, head_sums(width, count), count), head_spread(width, count))


def rms_rows(values):
    return values * lax.rsqrt(jnp.mean(values * values, axis=-1, keepdims=True) + EPS)


def head_masked(rows):
    head = iota(rows.shape, 1) // HEAD
    return jnp.concatenate([jnp.where(head == h, rows, 0.0).astype(BF) for h in range(4)], axis=0)


def head_merged(rows, count):
    head = iota((count, HALF), 1) // HEAD
    total = rows[:count]
    for h in range(1, 4):
        total = jnp.where(head == h, rows[h * count:(h + 1) * count], total)
    return total.astype(BF)


def first_kernel(l_ref, qkv_ref, occ_ref, kv_ref, cq_ref, out_ref, co_ref, lat_ref, far_ref, own_ref, share_ref, sent_ref):
    share_ref[...] = jnp.zeros(share_ref.shape, BF)
    rest = jnp.concatenate([out_ref[...], co_ref[...]], axis=0)
    share_ref[0:72, :] = rest[:, 0:PACK]
    share_ref[72:144, 0:256] = rest[:, PACK:]
    share_ref[72:144, 256:256 + INNER] = cq_ref[...]
    share_ref[REST:, 0:CHANNELS] = occ_ref[...]
    for q in range(4):
        at = slice(REST + 32 * q, REST + 32 * q + 32)
        share_ref[at, CHANNELS:CHANNELS + HALF] = kv_ref[:, q * HALF:(q + 1) * HALF]
    first = l_ref[0] == 0
    for n in range(3):
        low = qkv_ref[:, n * INNER:n * INNER + HALF]
        high = qkv_ref[:, n * INNER + HALF:(n + 1) * INNER]
        own_ref[:, n * HALF:(n + 1) * HALF] = jnp.where(first, low, high)
        far_ref[:, n * HALF:(n + 1) * HALF] = jnp.where(first, high, low)
    to, src = iota((192, 192), 0), iota((192, 192), 1)
    pick = onehot(src == (to // 8) % 3 * 64 + to // 24 * 8 + to % 8)
    rows = mm(pick, lat_ref[...]).astype(BF)
    sent_ref[0:192, :] = rows
    sent_ref[192:384, :] = rows


def prep_kernel(rows_ref, index_ref, normed_ref):
    normed = rms_rows(rows_ref[...].astype(F32)).astype(BF)
    for at in range(0, 1280, 256):
        spread = onehot(iota((WIDTH, 256), 0) == index_ref[:, at:at + 256])
        normed_ref[:, at:at + 256] = mm(normed, spread).astype(BF)


def temporal_kernel(normed_ref, own_ref, other_ref, mixed_ref):
    projected = mm(normed_ref[:, 0:INNER], own_ref[...]) + mm(
        normed_ref[:, 640:640 + INNER], other_ref[...]
    )
    both = head_normalize(projected[:, :INNER])
    query = both[:, :HALF]
    key = both[:, HALF:].astype(BF)
    value = projected[:, INNER:].astype(BF)
    live = iota((512, 128), 0) % 8 == iota((512, 128), 1) % 8
    for view in range(3):
        rows = slice(view * 128, view * 128 + 128)
        scores = mm_nt(head_masked(query[rows]), key[rows]) * SCALE
        exponent = jnp.where(live, jnp.exp(scores), 0.0)
        weights = (exponent * (1.0 / jnp.sum(exponent, axis=-1, keepdims=True))).astype(BF)
        mixed_ref[rows, :] = head_merged(mm(weights, value[rows]), 128)


def slab_kernel(yh_ref, a_ref, b_ref, slab_ref, rows_ref, held_ref, in_sem, out_sem):
    arrivals = []
    for n in range(16):
        side, x, c = n // 8, n // 2 % 4, n % 2
        yh = yh_ref[0] if side == 0 else 1 - yh_ref[0]
        to = pl.multiple_of((x * 4 + c) * SLAB + yh * (2 * SLAB), SLAB)
        src = (a_ref, b_ref)[side].at[pl.ds(n % 8 * SHARE + REST, SLAB)]
        arrivals.append(pltpu.make_async_copy(src, rows_ref.at[pl.ds(to, SLAB)], in_sem.at[n]))
        arrivals[-1].start()
    sums, spread = head_sums(640, HEADS), head_spread(640, HEADS)
    for copy in arrivals:
        copy.wait()
    quarters = []
    for q in range(4):
        parts = [rows_ref[n * SLAB + 32 * q:n * SLAB + 32 * q + 32, CHANNELS:CHANNELS + HALF] for n in range(16)]
        quarters.append(jnp.concatenate(parts, axis=0))
    weight = jnp.concatenate(quarters, axis=1)
    copies = []
    for part in range(8):
        rows = pl.ds(part * 256, 256)
        projected = mm(rows_ref[rows, 0:CHANNELS], weight)
        keys = projected[:, :640]
        held_ref[rows, 0:640] = (keys * mm(head_factors(keys, sums, HEADS), spread)).astype(BF)
        held_ref[rows, 640:] = projected[:, 640:].astype(BF)
        copies.append(pltpu.make_async_copy(held_ref.at[rows], slab_ref.at[rows], out_sem.at[part]))
        copies[-1].start()
    for copy in copies:
        copy.wait()


def cross_kernel(ids_ref, yh_ref, lat_ref, mixed_ref, live_ref, a_ref, b_ref, slab_ref,
                 result_ref, held_ref, picked_ref, out_ref, co_ref, cq_ref, sem):
    arrivals = []
    for n in range(16):
        yh = yh_ref[0] if n < 8 else 1 - yh_ref[0]
        to = pl.multiple_of(yh * (8 * REST) + n % 8 * REST, REST)
        src = (a_ref, b_ref)[n // 8].at[pl.ds(n % 8 * SHARE, REST)]
        arrivals.append(pltpu.make_async_copy(src, held_ref.at[pl.ds(to, REST)], sem.at[24 + n]))
        arrivals[-1].start()
    blocks = []
    for n in range(24):
        block = pl.ds(pl.multiple_of(ids_ref[n // 8, n % 8] * 64, 64), 64)
        blocks.append(pltpu.make_async_copy(slab_ref.at[block], picked_ref.at[pl.ds(n * 64, 64)], sem.at[n]))
        blocks[-1].start()

    to, src = iota((192, 192), 0), iota((192, 192), 1)
    pick = onehot(src == (to % 64) // 8 * 24 + to // 64 * 8 + to % 8)
    mixed = jnp.concatenate([mm(pick, mixed_ref[at:at + 192, :]) for at in (0, 192)], axis=1).astype(BF)
    for copy in arrivals:
        copy.wait()
    for n in range(16):
        x, yh, c = n // 4, n // 2 % 2, n % 2
        at = (yh * 8 + x * 2 + c) * REST
        to = slice(n * 36, n * 36 + 36)
        out_ref[to, 0:PACK] = held_ref[at:at + 36, :]
        co_ref[to, 0:PACK] = held_ref[at + 36:at + 72, :]
        out_ref[to, PACK:] = held_ref[at + 72:at + 108, 0:256]
        co_ref[to, PACK:] = held_ref[at + 108:at + 144, 0:256]
        cq_ref[n * 72:n * 72 + 72, :] = held_ref[at + 72:at + 144, 256:256 + INNER]
    hidden = (lat_ref[...].astype(F32) + mm(mixed, out_ref[...])).astype(BF)
    normed = rms_rows(hidden.astype(F32)).astype(BF)
    query = head_normalize(mm(normed, cq_ref[...]))
    query = jnp.concatenate([query, jnp.zeros((192, 64), F32)], axis=1)
    head = iota((64, 640), 1) // HEAD
    value_head = (iota((64, 640), 1) - 64 + HEAD) // HEAD - 1
    crossed = []
    for tile in range(3):
        for copy in blocks[tile * 8:tile * 8 + 8]:
            copy.wait()
        rows = query[tile * 64:tile * 64 + 64]
        masked = jnp.concatenate([jnp.where(head == h, rows, 0.0).astype(BF) for h in range(HEADS)], axis=0)
        keys = slice(tile * 512, tile * 512 + 512)
        scores = mm_nt(masked, picked_ref[keys, 0:640]) * SCALE
        exponent = jnp.exp(scores) * live_ref[tile:tile + 1, :]
        weights = (exponent * (1.0 / jnp.sum(exponent, axis=-1, keepdims=True))).astype(BF)
        mixed = mm(weights, picked_ref[keys, 512:WIDTH])
        total = mixed[:64]
        for h in range(1, HEADS):
            total = jnp.where(value_head == h, mixed[h * 64:h * 64 + 64], total)
        crossed.append(total)
    crossed = jnp.concatenate(crossed, axis=0)[:, 64:].astype(BF)
    result_ref[...] = (hidden.astype(F32) + mm(crossed, co_ref[...])).astype(BF)


def call(kernel, shapes, count, scalars=(), hbm=(), out_hbm=False, scratch=(), us=1, vmem=60):
    memory = [pltpu.SMEM if n in scalars else pl.ANY if n in hbm else pltpu.VMEM for n in range(count)]
    out_memory = pl.ANY if out_hbm else pltpu.VMEM
    return pl.pallas_call(
        kernel,
        out_shape=shapes,
        in_specs=[pl.BlockSpec(memory_space=m) for m in memory],
        out_specs=jax.tree.map(lambda _: pl.BlockSpec(memory_space=out_memory), shapes),
        scratch_shapes=scratch,
        compiler_params=pltpu.CompilerParams(vmem_limit_bytes=vmem * 1024 * 1024),
        cost_estimate=pl.CostEstimate(flops=us * 1150000000, bytes_accessed=us * 1000000, transcendentals=0),
    )


def after(values, *others):
    count = len(values)
    return lax.optimization_barrier(tuple(values) + others)[:count]


SWAP = [(0, 1), (1, 0)]
STEPS = (0, 1, 3, 2)


def along_x(block):
    return [block] + [lax.ppermute(block, "x", [(i, (i + s) % 4) for i in range(4)]) for s in STEPS[1:]]


def across_core(blocks):
    stacked = jnp.stack(blocks)
    return stacked, lax.ppermute(stacked, "c", SWAP)


def places(device, rows, pad):
    place = jnp.arange(2 * pad, dtype=jnp.int32)
    side, row = place // pad, place % pad
    x, yh, c = device(side, row // rows)
    start = ((x * 2 + yh) * 2 + c) * rows
    return jnp.where(row < 8 * rows, start + row % rows, -1).reshape(1, 2 * pad)


def shards(latents, block_mask, occupancy, temporal_qkv, temporal_out, cross_query, cross_keyval, cross_out):
    x, yh, c, l = (lax.axis_index(name) for name in ("x", "yh", "c", "l"))
    shape = jax.ShapeDtypeStruct
    lat = latents.reshape(192, WIDTH)

    def by_step(side, j):
        return (x - jnp.array(STEPS, jnp.int32)[jnp.minimum(j // 2, 3)] + 4) % 4, yh ^ (j % 2), c ^ side

    far, qkv, share, sent = call(
        first_kernel,
        (shape((72, 3 * HALF), BF), shape((72, 3 * HALF), BF), shape((SHARE, PACK), BF), shape((384, WIDTH), BF)),
        8, scalars=(0,), us=3,
    )(
        l.reshape(1).astype(jnp.int32), temporal_qkv, occupancy.reshape(128, CHANNELS), cross_keyval,
        cross_query, temporal_out, cross_out, lat,
    )

    def swap(block):
        return lax.ppermute(block, ("yh", "g", "l"), [(y, 7 - y) for y in range(8)])

    qkv_swapped, share_swapped = swap(far), swap(share)
    share_a = lax.all_gather(share, ("x", "c"), axis=0, tiled=True)
    time_rows = lax.all_to_all(
        sent.reshape(16, 24, WIDTH), ("l", "z"), split_axis=0, concat_axis=0, tiled=True
    ).reshape(384, WIDTH)
    own_blocks = along_x(qkv)
    share_swapped, qkv_swapped = after((share_swapped, qkv_swapped), time_rows, *own_blocks)
    normed = call(prep_kernel, shape((384, 1280), BF), 2, us=3, vmem=24)(time_rows, places(by_step, 72, 640))
    share_b = lax.all_gather(share_swapped, ("x", "c"), axis=0, tiled=True)
    pairs = zip(own_blocks, along_x(qkv_swapped))
    qkv_own, qkv_other = across_core([block for pair in pairs for block in pair])
    mixed = call(temporal_kernel, shape((384, HALF), BF), 3, us=5, vmem=24)(
        normed, qkv_own.reshape(INNER, 3 * HALF), qkv_other.reshape(INNER, 3 * HALF)
    )
    mixed_home = lax.all_to_all(
        mixed.reshape(16, 24, HALF), ("l", "z"), split_axis=0, concat_axis=0, tiled=True
    ).reshape(384, HALF)

    mask = block_mask[:, 0, :]
    rank = jnp.cumsum(mask, axis=1) - 1
    block = jnp.arange(32, dtype=jnp.int32)
    chosen = (rank[:, :, None] == jnp.arange(8, dtype=jnp.int32)) & (mask[:, :, None] > 0)
    ids = jnp.sum(jnp.where(chosen, block[None, :, None], 0), axis=1).astype(jnp.int32)
    live = jnp.repeat(jnp.any(chosen, axis=1), 64, axis=1).astype(F32)

    y_hi = yh.reshape(1).astype(jnp.int32)
    keys_values = call(
        slab_kernel, shape((2048, WIDTH), BF), 3, scalars=(0,), hbm=(1, 2), out_hbm=True, us=10,
        scratch=[
            pltpu.VMEM((2048, PACK), BF),
            pltpu.VMEM((2048, WIDTH), BF),
            pltpu.SemaphoreType.DMA((16,)),
            pltpu.SemaphoreType.DMA((8,)),
        ],
    )(y_hi, share_a, share_b)
    result = call(
        cross_kernel, shape((192, WIDTH), BF), 8, scalars=(0, 1), hbm=(5, 6, 7), us=10,
        scratch=[
            pltpu.VMEM((16 * REST, PACK), BF),
            pltpu.VMEM((24 * 64, WIDTH), BF),
            pltpu.VMEM((INNER, WIDTH), BF),
            pltpu.VMEM((INNER, WIDTH), BF),
            pltpu.VMEM((WIDTH, INNER), BF),
            pltpu.SemaphoreType.DMA((40,)),
        ],
    )(ids, y_hi, lat, mixed_home, live, share_a, share_b, keys_values)
    return result.reshape(latents.shape)


def solution(mesh):
    split = Mesh(mesh.devices.reshape(4, 2, 2, 2, 2, 8), ("x", "yh", "c", "g", "l", "z"))
    vox, vf = ("x", "yh", "c"), ("g", "l", "z")
    return jax.shard_map(
        shards,
        mesh=split,
        in_specs=(
            P(vf, vox, None),
            P(vf, vox, None),
            P(vox, None, None),
            P(vox, None),
            P(vox, None),
            P(vox, None),
            P(vox, None),
            P(vox, None),
        ),
        out_specs=P(vf, vox, None),
        check_vma=False,
    )
```

time: 126 us -> 124 us (0.984)
  starting transfers between devices: 39.3 us -> 50.8 us
  waiting for transfers between devices: 33.5 us -> 25 us
  Pallas kernels: 33.8 us -> 28.9 us
  other arithmetic: 3.46 us -> 1.23 us
    ppermute x1 -> x2, waiting for transfers between devices: 26.2 us -> 14.6 us  [swap(): return lax.ppermute(block, ('yh', 'g', 'l'), [(y, 7 - y) for y in range(8)])]
    ppermute x3 -> x6, starting transfers between devices: 9.94 us -> 19.7 us  [along_x(): lax.ppermute(block, 'x', [(i, (i + s) % 4) for i in range(4)])]
    pallas_call x4, Pallas kernels: 29.6 us -> 24.9 us  [the longest x1 10.9 us: shards(): call(cross_kernel, shape((192, WIDTH), BF), 8, scalars=(0, 1), hbm=(5, 6,...]
    all_gather x1, waiting for transfers between devices: 1.67 us -> 5.98 us  [shards(): share_b = lax.all_gather(share_swapped, ('x', 'c'), axis=0, tiled=True)]
    select_n x4 -> x1, other arithmetic: 2.13 us -> 0.16 us  [places(): return jnp.where(row < 8 * rows, start + row % rows, -1).reshape(1, 2 * pad)]
    ppermute x1 -> x2, starting transfers between devices: 5.15 us -> 7.07 us  [swap(): return lax.ppermute(block, ('yh', 'g', 'l'), [(y, 7 - y) for y in range(8)])]
    ppermute x3 -> x6, waiting for transfers between devices: 5.52 us -> 4.35 us  [along_x(): lax.ppermute(block, 'x', [(i, (i + s) % 4) for i in range(4)])]
    unnamed x7 -> x14, local copies, waits for them, and re-layouts: 1.62 us -> 2.53 us
  transfers between devices with their start and end apart: 9 -> 13, of which waited for: 4 -> 3; matrix products, arithmetic and copies ran while one was open for 3% -> 2% of each run, Pallas kernels for 15% -> 12%
where the time goes in v3:
time: 124 us; the launch traced here: 123 us
  starting transfers between devices  50.8 us (41%)
  Pallas kernels  28.9 us (23%)
  waiting for transfers between devices  25 us (20%)
  between operations  13.7 us (11%)
  local copies, waits for them, and re-layouts  3.3 us (3%)
    ppermute x6, starting transfers between devices, along_x(): lax.ppermute(block, 'x', [(i, (i + s) % 4) for i in range(4)])  19.7 us
    ppermute x2, waiting for transfers between devices, swap(): return lax.ppermute(block, ('yh', 'g', 'l'), [(y, 7 - y) for y in range(8)])  14.6 us
    all_to_all x1, starting transfers between devices, shards(): lax.all_to_all(sent.reshape(16, 24, WIDTH), ('l', 'z'), split_axis=0, con...  12 us
    pallas_call x1, Pallas kernels, shards(): call(cross_kernel, shape((192, WIDTH), BF), 8, scalars=(0, 1), hbm=(5, 6,...  10.9 us
    pallas_call x1, Pallas kernels, shards(): call(slab_kernel, shape((2048, WIDTH), BF), 3, scalars=(0,), hbm=(1, 2),...  9.32 us
    ppermute x2, starting transfers between devices, swap(): return lax.ppermute(block, ('yh', 'g', 'l'), [(y, 7 - y) for y in range(8)])  7.07 us
    all_to_all x1, starting transfers between devices, shards(): lax.all_to_all(mixed.reshape(16, 24, HALF), ('l', 'z'), split_axis=0, con...  6.49 us
    all_gather x1, waiting for transfers between devices, shards(): share_b = lax.all_gather(share_swapped, ('x', 'c'), axis=0, tiled=True)  5.98 us
  transfers between devices with their start and end apart: 13, of which 3 were waited for; matrix products, arithmetic and copies ran while one was open for 2% of the time, Pallas kernels for 12%

profile of v3, /device:TPU:1, one launch (start us, length us, event | category | flops | bytes accessed | tf_op | source)
XLA Modules:
  0.0 123.0 jit_solution(14607149877948951354)
XLA Ops:
  6.5 3.0 %shard_map.91 = (bf16[72,864]{1,0:T(8,128)(2,1)}, bf16[72,864]{1,0:T(8,128)(2,1)}, bf16[272,896]{1,0:T(8,128)(2,1)}, bf16[384,1152]{1,0:T(8,128)(2,1)}) custom-call(s32[1]{0:T(128)} %bitcast.2.l_ref, bf16[72,1728]{1,0:T(8,128)(2,1)} %qkv_ref.1, bf16[128,512]{1,0:T(8,128)(2,1)} %bitcast.46, bf16[32,1152]{1,0:T(8,128)(2,1)} %kv_ref.1, bf16[72,576]{1,0:T(8,128)(2,1)} %cq_ref.1, ...), custom_call_target="tpu_custom_call" | custom-call | flops 3449999872 | bytes 3000000 | tf_op jit(solution)/shard_map/pallas_call | solution.py:263
  9.6 12.0 %all-to-all-start = ((bf16[16,24,1152]{2,1,0:T(8,128)(2,1)}), bf16[16,24,1152]{2,1,0:T(8,128)(2,1)S(1)}, u32[]{:S(2)}, u32[]{:S(2)}) async-start(bf16[16,24,1152]{2,1,0:T(8,128)(2,1)} %bitcast.41), calls=%async_computation | async-start | bytes 1769472 | tf_op jit(solution)/shard_map/all_to_all | solution.py:277
  21.7 5.2 %collective-permute-start = (bf16[272,896]{1,0:T(8,128)(2,1)}, bf16[272,896]{1,0:T(8,128)(2,1)S(1)}, u32[]{:S(2)}, u32[]{:S(2)}) collective-permute-start(bf16[272,896]{1,0:T(8,128)(2,1)} %get-tuple-element.13), channel_id=1, source_target_pairs={{0,88},{8,80},{16,72},{24,64},{64,24},{72,16},{80,8},{88,0},{1,89}... | collective-permute-start | bytes 1462280 | tf_op jit(solution)/shard_map/ppermute | solution.py:273
  26.8 1.9 %collective-permute-start.1 = (bf16[72,864]{1,0:T(8,128)(2,1)}, bf16[72,864]{1,0:T(8,128)(2,1)S(1)}, u32[]{:S(2)}, u32[]{:S(2)}) collective-permute-start(bf16[72,864]{1,0:T(8,128)(2,1)} %get-tuple-element.14), channel_id=1, source_target_pairs={{0,88},{8,80},{16,72},{24,64},{64,24},{72,16},{80,8},{88,0},{1,89}... | collective-permute-start | bytes 373256 | tf_op jit(solution)/shard_map/ppermute | solution.py:273
  28.8 4.6 %collective-permute-start.4 = (bf16[72,864]{1,0:T(8,128)(2,1)}, bf16[72,864]{1,0:T(8,128)(2,1)S(1)}, u32[]{:S(2)}, u32[]{:S(2)}) collective-permute-start(bf16[72,864]{1,0:T(8,128)(2,1)} %get-tuple-element.12), channel_id=1, source_target_pairs={{0,256},{128,384},{256,0},{384,128},{1,257},{129,385},{257,1},{385... | collective-permute-start | bytes 373256 | tf_op jit(solution)/shard_map/ppermute | solution.py:239
  33.4 2.8 %collective-permute-start.3 = (bf16[72,864]{1,0:T(8,128)(2,1)}, bf16[72,864]{1,0:T(8,128)(2,1)S(1)}, u32[]{:S(2)}, u32[]{:S(2)}) collective-permute-start(bf16[72,864]{1,0:T(8,128)(2,1)} %get-tuple-element.12), channel_id=1, source_target_pairs={{0,384},{128,0},{256,128},{384,256},{1,385},{129,1},{257,129},{385... | collective-permute-start | bytes 373256 | tf_op jit(solution)/shard_map/ppermute | solution.py:239
  36.2 2.5 %collective-permute-start.2 = (bf16[72,864]{1,0:T(8,128)(2,1)}, bf16[72,864]{1,0:T(8,128)(2,1)S(1)}, u32[]{:S(2)}, u32[]{:S(2)}) collective-permute-start(bf16[72,864]{1,0:T(8,128)(2,1)} %get-tuple-element.12), channel_id=1, source_target_pairs={{0,128},{128,256},{256,384},{384,0},{1,129},{129,257},{257,385},{3... | collective-permute-start | bytes 373256 | tf_op jit(solution)/shard_map/ppermute | solution.py:239
  38.7 14.6 %collective-permute-done.1 = bf16[72,864]{1,0:T(8,128)(2,1)S(1)} collective-permute-done((bf16[72,864]{1,0:T(8,128)(2,1)}, bf16[72,864]{1,0:T(8,128)(2,1)S(1)}, u32[]{:S(2)}, u32[]{:S(2)}) %collective-permute-start.1) | collective-permute-done | bytes 124448 | tf_op jit(solution)/shard_map/ppermute | solution.py:273
  53.4 0.8 copy-done
  54.4 0.9 bitcast_dynamic-update-slice_fusion.7
  55.3 4.5 %collective-permute-start.7 = (bf16[72,864]{1,0:T(8,128)(2,1)S(1)}, bf16[72,864]{1,0:T(8,128)(2,1)S(1)}, u32[]{:S(2)}, u32[]{:S(2)}) collective-permute-start(bf16[72,864]{1,0:T(8,128)(2,1)S(1)} %collective-permute-done.1), channel_id=1, source_target_pairs={{0,256},{128,384},{256,0},{384,128},{1,257},{129,385},{257,1},{385... | collective-permute-start | bytes 373256 | tf_op jit(solution)/shard_map/ppermute | solution.py:239
  59.9 2.8 %collective-permute-start.6 = (bf16[72,864]{1,0:T(8,128)(2,1)S(1)}, bf16[72,864]{1,0:T(8,128)(2,1)S(1)}, u32[]{:S(2)}, u32[]{:S(2)}) collective-permute-start(bf16[72,864]{1,0:T(8,128)(2,1)S(1)} %collective-permute-done.1), channel_id=1, source_target_pairs={{0,384},{128,0},{256,128},{384,256},{1,385},{129,1},{257,129},{385... | collective-permute-start | bytes 373256 | tf_op jit(solution)/shard_map/ppermute | solution.py:239
  62.7 2.5 %collective-permute-start.5 = (bf16[72,864]{1,0:T(8,128)(2,1)S(1)}, bf16[72,864]{1,0:T(8,128)(2,1)S(1)}, u32[]{:S(2)}, u32[]{:S(2)}) collective-permute-start(bf16[72,864]{1,0:T(8,128)(2,1)S(1)} %collective-permute-done.1), channel_id=1, source_target_pairs={{0,128},{128,256},{256,384},{384,0},{1,129},{129,257},{257,385},{3... | collective-permute-start | bytes 373256 | tf_op jit(solution)/shard_map/ppermute | solution.py:239
  65.2 4.3 %collective-permute-done.5 = bf16[72,864]{1,0:T(8,128)(2,1)S(1)} collective-permute-done((bf16[72,864]{1,0:T(8,128)(2,1)S(1)}, bf16[72,864]{1,0:T(8,128)(2,1)S(1)}, u32[]{:S(2)}, u32[]{:S(2)}) %collective-permute-start.5) | collective-permute-done | bytes 124448 | tf_op jit(solution)/shard_map/ppermute | solution.py:239
  69.7 5.5 %collective-permute-start.8 = (bf16[8,72,864]{2,1,0:T(8,128)(2,1)S(1)}, bf16[8,72,864]{2,1,0:T(8,128)(2,1)S(1)}, u32[]{:S(2)}, u32[]{:S(2)}) collective-permute-start(bf16[8,72,864]{2,1,0:T(8,128)(2,1)S(1)} %bitcast_dynamic-update-slice_fusion), channel_id=1, source_target_pairs={{0,32},{32,0},{1,33},{33,1},{2,34},{34,2},{3,35},{35,3},{4,36},{36... | collective-permute-start | bytes 2985992 | tf_op jit(solution)/shard_map/ppermute | solution.py:244
  75.4 0.7 convert_element_type.6.live_ref
  76.1 0.7 select_reduce_fusion.ids_ref
  77.0 1.6 %shard_map.92.normed_ref = bf16[384,1280]{1,0:T(8,128)(2,1)S(1)} custom-call(bf16[384,1152]{1,0:T(8,128)(2,1)S(1)} %bitcast.38, s32[1,1280]{1,0:T(1,128)S(1)} %compare_select_fusion.8.index_ref), custom_call_target="tpu_custom_call" | custom-call | flops 3449999872 | bytes 3000000 | tf_op jit(solution)/shard_map/pallas_call | solution.py:282
  78.6 4.0 %shard_map.93 = bf16[384,288]{1,0:T(8,128)(2,1)} custom-call(bf16[384,1280]{1,0:T(8,128)(2,1)S(1)} %shard_map.92.normed_ref, bf16[576,864]{1,0:T(8,128)(2,1)S(1)} %bitcast.39, bf16[576,864]{1,0:T(8,128)(2,1)S(1)} %bitcast.40), custom_call_target="tpu_custom_call" | custom-call | flops 5750000128 | bytes 5000000 | tf_op jit(solution)/shard_map/pallas_call | solution.py:286
  82.7 6.5 %all-to-all-start.1 = ((bf16[16,24,288]{2,1,0:T(8,128)(2,1)}), bf16[16,24,288]{2,1,0:T(8,128)(2,1)S(1)}, u32[]{:S(2)}, u32[]{:S(2)}) async-start(bf16[16,24,288]{2,1,0:T(8,128)(2,1)} %bitcast.17), calls=%async_computation.1 | async-start | bytes 589824 | tf_op jit(solution)/shard_map/all_to_all | solution.py:289
  89.2 6.0 %all-gather.5.cloned.1.call-done.b_ref = bf16[2176,896]{1,0:T(8,128)(2,1)} async-done(((bf16[272,896]{1,0:T(8,128)(2,1)}), bf16[2176,896]{1,0:T(8,128)(2,1)}) %all-gather.5.cloned.1.call-update) | async-done | bytes 3899408 | tf_op jit(solution)/shard_map/all_gather | solution.py:283
  95.2 9.3 %shard_map.94.slab_ref = bf16[2048,1152]{1,0:T(8,128)(2,1)} custom-call(s32[1]{0:T(128)} %bitcast.yh_ref, bf16[2176,896]{1,0:T(8,128)(2,1)} %all-gather.3.cloned.1.call-done.a_ref, bf16[2176,896]{1,0:T(8,128)(2,1)} %all-gather.5.cloned.1.call-done.b_ref), custom_call_target="tpu_custom_call" | custom-call | flops 11500000256 | bytes 10000000 | tf_op jit(solution)/shard_map/pallas_call | solution.py:301
  104.5 0.7 copy-done.1
  105.2 10.9 %shard_map.95 = bf16[192,1152]{1,0:T(8,128)(2,1)} custom-call(s32[3,8]{1,0:T(4,128)} %select_reduce_fusion.ids_ref, s32[1]{0:T(128)} %bitcast.yh_ref, bf16[192,1152]{1,0:T(8,128)(2,1)} %bitcast.45, bf16[384,288]{1,0:T(8,128)(2,1)} %bitcast.42, f32[3,512]{1,0:T(4,128)} %convert_element_type.6.live_ref, bf16[2176,896]{1,0:T(8,128)(2,1)} %all-gather.3.cloned.1.call-done.a_ref, ...), custom_call_target="tpu_custom_call" | custom-call | flops 11500000256 | bytes 10000000 | tf_op jit(solution)/shard_map/pallas_call | solution.py:310
  (33 shorter events, 0.9 us)
Async XLA Ops:
  6.5 82.6 %all-gather.3.cloned.1.call-start = ((), (), s32[]{:S(2)}) async-start(), calls=%async_computation.2 | async-start | bytes 4386816 | tf_op jit(solution)/shard_map/all_gather | solution.py:276
  6.5 47.6 %copy-start.2 = (s32[3,1,32]{2,1,0:T(1,128)S(1)}, s32[3,1,32]{2,1,0:T(1,128)}, u32[]{:S(2)}) copy-start(s32[3,1,32]{2,1,0:T(1,128)} %param.10) | copy-start | bytes 1156
  9.6 43.8 %all-to-all-start = ((bf16[16,24,1152]{2,1,0:T(8,128)(2,1)}), bf16[16,24,1152]{2,1,0:T(8,128)(2,1)S(1)}, u32[]{:S(2)}, u32[]{:S(2)}) async-start(bf16[16,24,1152]{2,1,0:T(8,128)(2,1)} %bitcast.41), calls=%async_computation | async-start | bytes 1769472 | tf_op jit(solution)/shard_map/all_to_all | solution.py:277
  21.6 73.5 %all-gather.5.cloned.1.call-start = ((), (), s32[]{:S(2)}) async-start(), calls=%async_computation.3 | async-start | bytes 4386816 | tf_op jit(solution)/shard_map/all_gather | solution.py:283
  21.7 31.7 %collective-permute-start = (bf16[272,896]{1,0:T(8,128)(2,1)}, bf16[272,896]{1,0:T(8,128)(2,1)S(1)}, u32[]{:S(2)}, u32[]{:S(2)}) collective-permute-start(bf16[272,896]{1,0:T(8,128)(2,1)} %get-tuple-element.13), channel_id=1, source_target_pairs={{0,88},{8,80},{16,72},{24,64},{64,24},{72,16},{80,8},{88,0},{1,89}... | collective-permute-start | bytes 1462280 | tf_op jit(solution)/shard_map/ppermute | solution.py:273
  26.8 26.5 %collective-permute-start.1 = (bf16[72,864]{1,0:T(8,128)(2,1)}, bf16[72,864]{1,0:T(8,128)(2,1)S(1)}, u32[]{:S(2)}, u32[]{:S(2)}) collective-permute-start(bf16[72,864]{1,0:T(8,128)(2,1)} %get-tuple-element.14), channel_id=1, source_target_pairs={{0,88},{8,80},{16,72},{24,64},{64,24},{72,16},{80,8},{88,0},{1,89}... | collective-permute-start | bytes 373256 | tf_op jit(solution)/shard_map/ppermute | solution.py:273
  28.8 24.6 %collective-permute-start.4 = (bf16[72,864]{1,0:T(8,128)(2,1)}, bf16[72,864]{1,0:T(8,128)(2,1)S(1)}, u32[]{:S(2)}, u32[]{:S(2)}) collective-permute-start(bf16[72,864]{1,0:T(8,128)(2,1)} %get-tuple-element.12), channel_id=1, source_target_pairs={{0,256},{128,384},{256,0},{384,128},{1,257},{129,385},{257,1},{385... | collective-permute-start | bytes 373256 | tf_op jit(solution)/shard_map/ppermute | solution.py:239
  33.4 19.9 %collective-permute-start.3 = (bf16[72,864]{1,0:T(8,128)(2,1)}, bf16[72,864]{1,0:T(8,128)(2,1)S(1)}, u32[]{:S(2)}, u32[]{:S(2)}) collective-permute-start(bf16[72,864]{1,0:T(8,128)(2,1)} %get-tuple-element.12), channel_id=1, source_target_pairs={{0,384},{128,0},{256,128},{384,256},{1,385},{129,1},{257,129},{385... | collective-permute-start | bytes 373256 | tf_op jit(solution)/shard_map/ppermute | solution.py:239
  36.2 17.1 %collective-permute-start.2 = (bf16[72,864]{1,0:T(8,128)(2,1)}, bf16[72,864]{1,0:T(8,128)(2,1)S(1)}, u32[]{:S(2)}, u32[]{:S(2)}) collective-permute-start(bf16[72,864]{1,0:T(8,128)(2,1)} %get-tuple-element.12), channel_id=1, source_target_pairs={{0,128},{128,256},{256,384},{384,0},{1,129},{129,257},{257,385},{3... | collective-permute-start | bytes 373256 | tf_op jit(solution)/shard_map/ppermute | solution.py:239
  53.3 0.8 copy-start
  55.3 14.3 %collective-permute-start.7 = (bf16[72,864]{1,0:T(8,128)(2,1)S(1)}, bf16[72,864]{1,0:T(8,128)(2,1)S(1)}, u32[]{:S(2)}, u32[]{:S(2)}) collective-permute-start(bf16[72,864]{1,0:T(8,128)(2,1)S(1)} %collective-permute-done.1), channel_id=1, source_target_pairs={{0,256},{128,384},{256,0},{384,128},{1,257},{129,385},{257,1},{385... | collective-permute-start | bytes 373256 | tf_op jit(solution)/shard_map/ppermute | solution.py:239
  59.9 9.7 %collective-permute-start.6 = (bf16[72,864]{1,0:T(8,128)(2,1)S(1)}, bf16[72,864]{1,0:T(8,128)(2,1)S(1)}, u32[]{:S(2)}, u32[]{:S(2)}) collective-permute-start(bf16[72,864]{1,0:T(8,128)(2,1)S(1)} %collective-permute-done.1), channel_id=1, source_target_pairs={{0,384},{128,0},{256,128},{384,256},{1,385},{129,1},{257,129},{385... | collective-permute-start | bytes 373256 | tf_op jit(solution)/shard_map/ppermute | solution.py:239
  62.7 6.9 %collective-permute-start.5 = (bf16[72,864]{1,0:T(8,128)(2,1)S(1)}, bf16[72,864]{1,0:T(8,128)(2,1)S(1)}, u32[]{:S(2)}, u32[]{:S(2)}) collective-permute-start(bf16[72,864]{1,0:T(8,128)(2,1)S(1)} %collective-permute-done.1), channel_id=1, source_target_pairs={{0,128},{128,256},{256,384},{384,0},{1,129},{129,257},{257,385},{3... | collective-permute-start | bytes 373256 | tf_op jit(solution)/shard_map/ppermute | solution.py:239
  69.7 8.9 %collective-permute-start.8 = (bf16[8,72,864]{2,1,0:T(8,128)(2,1)S(1)}, bf16[8,72,864]{2,1,0:T(8,128)(2,1)S(1)}, u32[]{:S(2)}, u32[]{:S(2)}) collective-permute-start(bf16[8,72,864]{2,1,0:T(8,128)(2,1)S(1)} %bitcast_dynamic-update-slice_fusion), channel_id=1, source_target_pairs={{0,32},{32,0},{1,33},{33,1},{2,34},{34,2},{3,35},{35,3},{4,36},{36... | collective-permute-start | bytes 2985992 | tf_op jit(solution)/shard_map/ppermute | solution.py:244
  82.7 21.8 %all-to-all-start.1 = ((bf16[16,24,288]{2,1,0:T(8,128)(2,1)}), bf16[16,24,288]{2,1,0:T(8,128)(2,1)S(1)}, u32[]{:S(2)}, u32[]{:S(2)}) async-start(bf16[16,24,288]{2,1,0:T(8,128)(2,1)} %bitcast.17), calls=%async_computation.1 | async-start | bytes 589824 | tf_op jit(solution)/shard_map/all_to_all | solution.py:289
  104.5 0.7 copy-start.1
Sparse Core Ops, SparseCore 0:
  9.7 47.6 all-gather.2
  59.5 35.5 all-gather.4

commit v4 on v3

--- a/solution.py
+++ b/solution.py
@@ -81,7 +81,7 @@
     return total.astype(BF)
 
 
-def first_kernel(l_ref, qkv_ref, occ_ref, kv_ref, cq_ref, out_ref, co_ref, lat_ref, far_ref, own_ref, share_ref, sent_ref):
+def share_kernel(occ_ref, kv_ref, cq_ref, out_ref, co_ref, share_ref):
     share_ref[...] = jnp.zeros(share_ref.shape, BF)
     rest = jnp.concatenate([out_ref[...], co_ref[...]], axis=0)
     share_ref[0:72, :] = rest[:, 0:PACK]
@@ -91,6 +91,9 @@
     for q in range(4):
         at = slice(REST + 32 * q, REST + 32 * q + 32)
         share_ref[at, CHANNELS:CHANNELS + HALF] = kv_ref[:, q * HALF:(q + 1) * HALF]
+
+
+def send_kernel(l_ref, qkv_ref, lat_ref, far_ref, own_ref, sent_ref):
     first = l_ref[0] == 0
     for n in range(3):
         low = qkv_ref[:, n * INNER:n * INNER + HALF]
@@ -146,8 +149,8 @@
         quarters.append(jnp.concatenate(parts, axis=0))
     weight = jnp.concatenate(quarters, axis=1)
     copies = []
-    for part in range(8):
-        rows = pl.ds(part * 256, 256)
+    for part in range(4):
+        rows = pl.ds(part * 512, 512)
         projected = mm(rows_ref[rows, 0:CHANNELS], weight)
         keys = projected[:, :640]
         held_ref[rows, 0:640] = (keys * mm(head_factors(keys, sums, HEADS), spread)).astype(BF)
@@ -260,14 +263,14 @@
     def by_step(side, j):
         return (x - jnp.array(STEPS, jnp.int32)[jnp.minimum(j // 2, 3)] + 4) % 4, yh ^ (j % 2), c ^ side
 
-    far, qkv, share, sent = call(
-        first_kernel,
-        (shape((72, 3 * HALF), BF), shape((72, 3 * HALF), BF), shape((SHARE, PACK), BF), shape((384, WIDTH), BF)),
-        8, scalars=(0,), us=3,
-    )(
-        l.reshape(1).astype(jnp.int32), temporal_qkv, occupancy.reshape(128, CHANNELS), cross_keyval,
-        cross_query, temporal_out, cross_out, lat,
-    )
+    share = call(share_kernel, shape((SHARE, PACK), BF), 5, us=2)(
+        occupancy.reshape(128, CHANNELS), cross_keyval, cross_query, temporal_out, cross_out
+    )
+    far, qkv, sent = call(
+        send_kernel,
+        (shape((72, 3 * HALF), BF), shape((72, 3 * HALF), BF), shape((384, WIDTH), BF)),
+        3, scalars=(0,), us=2,
+    )(l.reshape(1).astype(jnp.int32), temporal_qkv, lat)
 
     def swap(block):
         return lax.ppermute(block, ("yh", "g", "l"), [(y, 7 - y) for y in range(8)])
@@ -304,7 +307,7 @@
             pltpu.VMEM((2048, PACK), BF),
             pltpu.VMEM((2048, WIDTH), BF),
             pltpu.SemaphoreType.DMA((16,)),
-            pltpu.SemaphoreType.DMA((8,)),
+            pltpu.SemaphoreType.DMA((4,)),
         ],
     )(y_hi, share_a, share_b)
     result = call(

time: 124 us -> 124 us (level)
    pallas_call x1 -> x2, Pallas kernels: 3.04 us -> 4.54 us  [the longest x1 2.59 us: shards(): call(send_kernel, (shape((72, 3 * HALF), BF), shape((72, 3 * HALF), BF),...]
    unnamed x14 -> x16, local copies, waits for them, and re-layouts: 2.53 us -> 2.52 us
  transfers between devices with their start and end apart: 13 -> 13, of which waited for: 3 -> 3; matrix products, arithmetic and copies ran while one was open for 2% -> 2% of each run, Pallas kernels for 12% -> 14%
where the time goes in v4:
time: 124 us; the launch traced here: 123 us
  starting transfers between devices  50.8 us (41%)
  Pallas kernels  30 us (24%)
  waiting for transfers between devices  23.8 us (19%)
  between operations  13.7 us (11%)
  local copies, waits for them, and re-layouts  3.3 us (3%)
  other arithmetic  1.25 us (1%)
    ppermute x6, starting transfers between devices, along_x(): lax.ppermute(block, 'x', [(i, (i + s) % 4) for i in range(4)])  19.8 us
    ppermute x2, waiting for transfers between devices, swap(): return lax.ppermute(block, ('yh', 'g', 'l'), [(y, 7 - y) for y in range(8)])  14.4 us
    all_to_all x1, starting transfers between devices, shards(): lax.all_to_all(sent.reshape(16, 24, WIDTH), ('l', 'z'), split_axis=0, con...  12 us
    pallas_call x1, Pallas kernels, shards(): call(cross_kernel, shape((192, WIDTH), BF), 8, scalars=(0, 1), hbm=(5, 6,...  10.9 us
    pallas_call x1, Pallas kernels, shards(): call(slab_kernel, shape((2048, WIDTH), BF), 3, scalars=(0,), hbm=(1, 2),...  8.88 us
    ppermute x2, starting transfers between devices, swap(): return lax.ppermute(block, ('yh', 'g', 'l'), [(y, 7 - y) for y in range(8)])  7.08 us
    all_to_all x1, starting transfers between devices, shards(): lax.all_to_all(mixed.reshape(16, 24, HALF), ('l', 'z'), split_axis=0, con...  6.48 us
    ppermute x1, starting transfers between devices, across_core(): return (stacked, lax.ppermute(stacked, 'c', SWAP))  5.49 us
  transfers between devices with their start and end apart: 13, of which 3 were waited for; matrix products, arithmetic and copies ran while one was open for 2% of the time, Pallas kernels for 14%

profile of v4, /device:TPU:1, one launch (start us, length us, event | category | flops | bytes accessed | tf_op | source)
XLA Modules:
  0.0 122.9 jit_solution(5443026436715865994)
XLA Ops:
  6.5 2.0 %shard_map.93 = bf16[272,896]{1,0:T(8,128)(2,1)} custom-call(bf16[128,512]{1,0:T(8,128)(2,1)} %bitcast.46, bf16[32,1152]{1,0:T(8,128)(2,1)} %kv_ref.1, bf16[72,576]{1,0:T(8,128)(2,1)} %cq_ref.1, bf16[36,1152]{1,0:T(8,128)(2,1)} %out_ref.1, bf16[36,1152]{1,0:T(8,128)(2,1)} %co_ref.1), custom_call_target="tpu_custom_call" | custom-call | flops 2300000000 | bytes 2000000 | tf_op jit(solution)/shard_map/pallas_call | solution.py:266
  8.5 2.6 %shard_map.91 = (bf16[72,864]{1,0:T(8,128)(2,1)}, bf16[72,864]{1,0:T(8,128)(2,1)}, bf16[384,1152]{1,0:T(8,128)(2,1)}) custom-call(s32[1]{0:T(128)} %bitcast.2.l_ref, bf16[72,1728]{1,0:T(8,128)(2,1)} %qkv_ref.1, bf16[192,1152]{1,0:T(8,128)(2,1)} %bitcast.44), custom_call_target="tpu_custom_call" | custom-call | flops 2300000000 | bytes 2000000 | tf_op jit(solution)/shard_map/pallas_call | solution.py:269
  11.1 12.0 %all-to-all-start = ((bf16[16,24,1152]{2,1,0:T(8,128)(2,1)}), bf16[16,24,1152]{2,1,0:T(8,128)(2,1)S(1)}, u32[]{:S(2)}, u32[]{:S(2)}) async-start(bf16[16,24,1152]{2,1,0:T(8,128)(2,1)} %bitcast.41), calls=%async_computation | async-start | bytes 1769472 | tf_op jit(solution)/shard_map/all_to_all | solution.py:280
  23.2 5.2 %collective-permute-start = (bf16[272,896]{1,0:T(8,128)(2,1)S(1)}, bf16[272,896]{1,0:T(8,128)(2,1)S(1)}, u32[]{:S(2)}, u32[]{:S(2)}) collective-permute-start(bf16[272,896]{1,0:T(8,128)(2,1)S(1)} %copy-done), channel_id=1, source_target_pairs={{0,88},{8,80},{16,72},{24,64},{64,24},{72,16},{80,8},{88,0},{1,89}... | collective-permute-start | bytes 1462280 | tf_op jit(solution)/shard_map/ppermute | solution.py:276
  28.4 1.9 %collective-permute-start.1 = (bf16[72,864]{1,0:T(8,128)(2,1)}, bf16[72,864]{1,0:T(8,128)(2,1)S(1)}, u32[]{:S(2)}, u32[]{:S(2)}) collective-permute-start(bf16[72,864]{1,0:T(8,128)(2,1)} %get-tuple-element.12), channel_id=1, source_target_pairs={{0,88},{8,80},{16,72},{24,64},{64,24},{72,16},{80,8},{88,0},{1,89}... | collective-permute-start | bytes 373256 | tf_op jit(solution)/shard_map/ppermute | solution.py:276
  30.3 4.7 %collective-permute-start.4 = (bf16[72,864]{1,0:T(8,128)(2,1)}, bf16[72,864]{1,0:T(8,128)(2,1)S(1)}, u32[]{:S(2)}, u32[]{:S(2)}) collective-permute-start(bf16[72,864]{1,0:T(8,128)(2,1)} %get-tuple-element.11), channel_id=1, source_target_pairs={{0,256},{128,384},{256,0},{384,128},{1,257},{129,385},{257,1},{385... | collective-permute-start | bytes 373256 | tf_op jit(solution)/shard_map/ppermute | solution.py:242
  34.9 2.8 %collective-permute-start.3 = (bf16[72,864]{1,0:T(8,128)(2,1)}, bf16[72,864]{1,0:T(8,128)(2,1)S(1)}, u32[]{:S(2)}, u32[]{:S(2)}) collective-permute-start(bf16[72,864]{1,0:T(8,128)(2,1)} %get-tuple-element.11), channel_id=1, source_target_pairs={{0,384},{128,0},{256,128},{384,256},{1,385},{129,1},{257,129},{385... | collective-permute-start | bytes 373256 | tf_op jit(solution)/shard_map/ppermute | solution.py:242
  37.7 2.5 %collective-permute-start.2 = (bf16[72,864]{1,0:T(8,128)(2,1)}, bf16[72,864]{1,0:T(8,128)(2,1)S(1)}, u32[]{:S(2)}, u32[]{:S(2)}) collective-permute-start(bf16[72,864]{1,0:T(8,128)(2,1)} %get-tuple-element.11), channel_id=1, source_target_pairs={{0,128},{128,256},{256,384},{384,0},{1,129},{129,257},{257,385},{3... | collective-permute-start | bytes 373256 | tf_op jit(solution)/shard_map/ppermute | solution.py:242
  40.2 14.4 %collective-permute-done.1 = bf16[72,864]{1,0:T(8,128)(2,1)S(1)} collective-permute-done((bf16[72,864]{1,0:T(8,128)(2,1)}, bf16[72,864]{1,0:T(8,128)(2,1)S(1)}, u32[]{:S(2)}, u32[]{:S(2)}) %collective-permute-start.1) | collective-permute-done | bytes 124448 | tf_op jit(solution)/shard_map/ppermute | solution.py:276
  54.7 0.8 copy-done.1
  55.7 0.9 bitcast_dynamic-update-slice_fusion.7
  56.6 4.6 %collective-permute-start.7 = (bf16[72,864]{1,0:T(8,128)(2,1)S(1)}, bf16[72,864]{1,0:T(8,128)(2,1)S(1)}, u32[]{:S(2)}, u32[]{:S(2)}) collective-permute-start(bf16[72,864]{1,0:T(8,128)(2,1)S(1)} %collective-permute-done.1), channel_id=1, source_target_pairs={{0,256},{128,384},{256,0},{384,128},{1,257},{129,385},{257,1},{385... | collective-permute-start | bytes 373256 | tf_op jit(solution)/shard_map/ppermute | solution.py:242
  61.2 2.8 %collective-permute-start.6 = (bf16[72,864]{1,0:T(8,128)(2,1)S(1)}, bf16[72,864]{1,0:T(8,128)(2,1)S(1)}, u32[]{:S(2)}, u32[]{:S(2)}) collective-permute-start(bf16[72,864]{1,0:T(8,128)(2,1)S(1)} %collective-permute-done.1), channel_id=1, source_target_pairs={{0,384},{128,0},{256,128},{384,256},{1,385},{129,1},{257,129},{385... | collective-permute-start | bytes 373256 | tf_op jit(solution)/shard_map/ppermute | solution.py:242
  64.0 2.5 %collective-permute-start.5 = (bf16[72,864]{1,0:T(8,128)(2,1)S(1)}, bf16[72,864]{1,0:T(8,128)(2,1)S(1)}, u32[]{:S(2)}, u32[]{:S(2)}) collective-permute-start(bf16[72,864]{1,0:T(8,128)(2,1)S(1)} %collective-permute-done.1), channel_id=1, source_target_pairs={{0,128},{128,256},{256,384},{384,0},{1,129},{129,257},{257,385},{3... | collective-permute-start | bytes 373256 | tf_op jit(solution)/shard_map/ppermute | solution.py:242
  66.5 4.3 %collective-permute-done.5 = bf16[72,864]{1,0:T(8,128)(2,1)S(1)} collective-permute-done((bf16[72,864]{1,0:T(8,128)(2,1)S(1)}, bf16[72,864]{1,0:T(8,128)(2,1)S(1)}, u32[]{:S(2)}, u32[]{:S(2)}) %collective-permute-start.5) | collective-permute-done | bytes 124448 | tf_op jit(solution)/shard_map/ppermute | solution.py:242
  71.0 5.5 %collective-permute-start.8 = (bf16[8,72,864]{2,1,0:T(8,128)(2,1)S(1)}, bf16[8,72,864]{2,1,0:T(8,128)(2,1)S(1)}, u32[]{:S(2)}, u32[]{:S(2)}) collective-permute-start(bf16[8,72,864]{2,1,0:T(8,128)(2,1)S(1)} %bitcast_dynamic-update-slice_fusion), channel_id=1, source_target_pairs={{0,32},{32,0},{1,33},{33,1},{2,34},{34,2},{3,35},{35,3},{4,36},{36... | collective-permute-start | bytes 2985992 | tf_op jit(solution)/shard_map/ppermute | solution.py:247
  77.4 0.7 select_reduce_fusion.ids_ref
  78.3 1.6 %shard_map.92.normed_ref = bf16[384,1280]{1,0:T(8,128)(2,1)S(1)} custom-call(bf16[384,1152]{1,0:T(8,128)(2,1)S(1)} %bitcast.38, s32[1,1280]{1,0:T(1,128)S(1)} %compare_select_fusion.8.index_ref), custom_call_target="tpu_custom_call" | custom-call | flops 3449999872 | bytes 3000000 | tf_op jit(solution)/shard_map/pallas_call | solution.py:285
  79.9 4.0 %shard_map.94 = bf16[384,288]{1,0:T(8,128)(2,1)} custom-call(bf16[384,1280]{1,0:T(8,128)(2,1)S(1)} %shard_map.92.normed_ref, bf16[576,864]{1,0:T(8,128)(2,1)S(1)} %bitcast.39, bf16[576,864]{1,0:T(8,128)(2,1)S(1)} %bitcast.40), custom_call_target="tpu_custom_call" | custom-call | flops 5750000128 | bytes 5000000 | tf_op jit(solution)/shard_map/pallas_call | solution.py:289
  84.0 6.5 %all-to-all-start.1 = ((bf16[16,24,288]{2,1,0:T(8,128)(2,1)}), bf16[16,24,288]{2,1,0:T(8,128)(2,1)S(1)}, u32[]{:S(2)}, u32[]{:S(2)}) async-start(bf16[16,24,288]{2,1,0:T(8,128)(2,1)} %bitcast.17), calls=%async_computation.1 | async-start | bytes 589824 | tf_op jit(solution)/shard_map/all_to_all | solution.py:292
  90.5 5.0 %all-gather.5.cloned.1.call-done.b_ref = bf16[2176,896]{1,0:T(8,128)(2,1)} async-done(((bf16[272,896]{1,0:T(8,128)(2,1)}), bf16[2176,896]{1,0:T(8,128)(2,1)}) %all-gather.5.cloned.1.call-update) | async-done | bytes 3899408 | tf_op jit(solution)/shard_map/all_gather | solution.py:286
  95.5 8.9 %shard_map.95.slab_ref = bf16[2048,1152]{1,0:T(8,128)(2,1)} custom-call(s32[1]{0:T(128)} %bitcast.yh_ref, bf16[2176,896]{1,0:T(8,128)(2,1)} %all-gather.3.cloned.1.call-done.a_ref, bf16[2176,896]{1,0:T(8,128)(2,1)} %all-gather.5.cloned.1.call-done.b_ref), custom_call_target="tpu_custom_call" | custom-call | flops 11500000256 | bytes 10000000 | tf_op jit(solution)/shard_map/pallas_call | solution.py:304
  104.4 0.7 copy-done.2
  105.1 10.9 %shard_map.96 = bf16[192,1152]{1,0:T(8,128)(2,1)} custom-call(s32[3,8]{1,0:T(4,128)} %select_reduce_fusion.ids_ref, s32[1]{0:T(128)} %bitcast.yh_ref, bf16[192,1152]{1,0:T(8,128)(2,1)} %bitcast.45, bf16[384,288]{1,0:T(8,128)(2,1)} %bitcast.42, f32[3,512]{1,0:T(4,128)} %convert_element_type.6.live_ref, bf16[2176,896]{1,0:T(8,128)(2,1)} %all-gather.3.cloned.1.call-done.a_ref, ...), custom_call_target="tpu_custom_call" | custom-call | flops 11500000256 | bytes 10000000 | tf_op jit(solution)/shard_map/pallas_call | solution.py:313
  (36 shorter events, 1.6 us)
Async XLA Ops:
  6.5 84.0 %all-gather.3.cloned.1.call-start = ((), (), s32[]{:S(2)}) async-start(), calls=%async_computation.2 | async-start | bytes 4386816 | tf_op jit(solution)/shard_map/all_gather | solution.py:279
  8.5 14.7 %copy-start = (bf16[272,896]{1,0:T(8,128)(2,1)S(1)}, bf16[272,896]{1,0:T(8,128)(2,1)}, u32[]{:S(2)}) copy-start(bf16[272,896]{1,0:T(8,128)(2,1)} %shard_map.93) | copy-start | bytes 1462276
  8.5 46.9 %copy-start.3 = (s32[3,1,32]{2,1,0:T(1,128)S(1)}, s32[3,1,32]{2,1,0:T(1,128)}, u32[]{:S(2)}) copy-start(s32[3,1,32]{2,1,0:T(1,128)} %param.10) | copy-start | bytes 1156
  11.1 43.5 %all-to-all-start = ((bf16[16,24,1152]{2,1,0:T(8,128)(2,1)}), bf16[16,24,1152]{2,1,0:T(8,128)(2,1)S(1)}, u32[]{:S(2)}, u32[]{:S(2)}) async-start(bf16[16,24,1152]{2,1,0:T(8,128)(2,1)} %bitcast.41), calls=%async_computation | async-start | bytes 1769472 | tf_op jit(solution)/shard_map/all_to_all | solution.py:280
  23.1 72.4 %all-gather.5.cloned.1.call-start = ((), (), s32[]{:S(2)}) async-start(), calls=%async_computation.3 | async-start | bytes 4386816 | tf_op jit(solution)/shard_map/all_gather | solution.py:286
  23.2 31.5 %collective-permute-start = (bf16[272,896]{1,0:T(8,128)(2,1)S(1)}, bf16[272,896]{1,0:T(8,128)(2,1)S(1)}, u32[]{:S(2)}, u32[]{:S(2)}) collective-permute-start(bf16[272,896]{1,0:T(8,128)(2,1)S(1)} %copy-done), channel_id=1, source_target_pairs={{0,88},{8,80},{16,72},{24,64},{64,24},{72,16},{80,8},{88,0},{1,89}... | collective-permute-start | bytes 1462280 | tf_op jit(solution)/shard_map/ppermute | solution.py:276
  28.4 26.3 %collective-permute-start.1 = (bf16[72,864]{1,0:T(8,128)(2,1)}, bf16[72,864]{1,0:T(8,128)(2,1)S(1)}, u32[]{:S(2)}, u32[]{:S(2)}) collective-permute-start(bf16[72,864]{1,0:T(8,128)(2,1)} %get-tuple-element.12), channel_id=1, source_target_pairs={{0,88},{8,80},{16,72},{24,64},{64,24},{72,16},{80,8},{88,0},{1,89}... | collective-permute-start | bytes 373256 | tf_op jit(solution)/shard_map/ppermute | solution.py:276
  30.3 24.4 %collective-permute-start.4 = (bf16[72,864]{1,0:T(8,128)(2,1)}, bf16[72,864]{1,0:T(8,128)(2,1)S(1)}, u32[]{:S(2)}, u32[]{:S(2)}) collective-permute-start(bf16[72,864]{1,0:T(8,128)(2,1)} %get-tuple-element.11), channel_id=1, source_target_pairs={{0,256},{128,384},{256,0},{384,128},{1,257},{129,385},{257,1},{385... | collective-permute-start | bytes 373256 | tf_op jit(solution)/shard_map/ppermute | solution.py:242
  34.9 19.7 %collective-permute-start.3 = (bf16[72,864]{1,0:T(8,128)(2,1)}, bf16[72,864]{1,0:T(8,128)(2,1)S(1)}, u32[]{:S(2)}, u32[]{:S(2)}) collective-permute-start(bf16[72,864]{1,0:T(8,128)(2,1)} %get-tuple-element.11), channel_id=1, source_target_pairs={{0,384},{128,0},{256,128},{384,256},{1,385},{129,1},{257,129},{385... | collective-permute-start | bytes 373256 | tf_op jit(solution)/shard_map/ppermute | solution.py:242
  37.7 16.9 %collective-permute-start.2 = (bf16[72,864]{1,0:T(8,128)(2,1)}, bf16[72,864]{1,0:T(8,128)(2,1)S(1)}, u32[]{:S(2)}, u32[]{:S(2)}) collective-permute-start(bf16[72,864]{1,0:T(8,128)(2,1)} %get-tuple-element.11), channel_id=1, source_target_pairs={{0,128},{128,256},{256,384},{384,0},{1,129},{129,257},{257,385},{3... | collective-permute-start | bytes 373256 | tf_op jit(solution)/shard_map/ppermute | solution.py:242
  54.7 0.8 copy-start.1
  56.6 14.3 %collective-permute-start.7 = (bf16[72,864]{1,0:T(8,128)(2,1)S(1)}, bf16[72,864]{1,0:T(8,128)(2,1)S(1)}, u32[]{:S(2)}, u32[]{:S(2)}) collective-permute-start(bf16[72,864]{1,0:T(8,128)(2,1)S(1)} %collective-permute-done.1), channel_id=1, source_target_pairs={{0,256},{128,384},{256,0},{384,128},{1,257},{129,385},{257,1},{385... | collective-permute-start | bytes 373256 | tf_op jit(solution)/shard_map/ppermute | solution.py:242
  61.2 9.7 %collective-permute-start.6 = (bf16[72,864]{1,0:T(8,128)(2,1)S(1)}, bf16[72,864]{1,0:T(8,128)(2,1)S(1)}, u32[]{:S(2)}, u32[]{:S(2)}) collective-permute-start(bf16[72,864]{1,0:T(8,128)(2,1)S(1)} %collective-permute-done.1), channel_id=1, source_target_pairs={{0,384},{128,0},{256,128},{384,256},{1,385},{129,1},{257,129},{385... | collective-permute-start | bytes 373256 | tf_op jit(solution)/shard_map/ppermute | solution.py:242
  64.0 6.9 %collective-permute-start.5 = (bf16[72,864]{1,0:T(8,128)(2,1)S(1)}, bf16[72,864]{1,0:T(8,128)(2,1)S(1)}, u32[]{:S(2)}, u32[]{:S(2)}) collective-permute-start(bf16[72,864]{1,0:T(8,128)(2,1)S(1)} %collective-permute-done.1), channel_id=1, source_target_pairs={{0,128},{128,256},{256,384},{384,0},{1,129},{129,257},{257,385},{3... | collective-permute-start | bytes 373256 | tf_op jit(solution)/shard_map/ppermute | solution.py:242
  71.0 8.9 %collective-permute-start.8 = (bf16[8,72,864]{2,1,0:T(8,128)(2,1)S(1)}, bf16[8,72,864]{2,1,0:T(8,128)(2,1)S(1)}, u32[]{:S(2)}, u32[]{:S(2)}) collective-permute-start(bf16[8,72,864]{2,1,0:T(8,128)(2,1)S(1)} %bitcast_dynamic-update-slice_fusion), channel_id=1, source_target_pairs={{0,32},{32,0},{1,33},{33,1},{2,34},{34,2},{3,35},{35,3},{4,36},{36... | collective-permute-start | bytes 2985992 | tf_op jit(solution)/shard_map/ppermute | solution.py:247
  84.0 20.4 %all-to-all-start.1 = ((bf16[16,24,288]{2,1,0:T(8,128)(2,1)}), bf16[16,24,288]{2,1,0:T(8,128)(2,1)S(1)}, u32[]{:S(2)}, u32[]{:S(2)}) async-start(bf16[16,24,288]{2,1,0:T(8,128)(2,1)} %bitcast.17), calls=%async_computation.1 | async-start | bytes 589824 | tf_op jit(solution)/shard_map/all_to_all | solution.py:292
  104.4 0.7 copy-start.2
Sparse Core Ops, SparseCore 0:
  9.5 47.6 all-gather.2
  59.3 36.1 all-gather.4
